TPU v7x, 256 devices: a whole 4x4x8 slice. The times are simulated.
256 devices in a mesh: tm: 64 (over z, y, core), col: 4 (over x).
Axes of the slice: x: 4, y: 4, z: 8, core: 2. Of those that a mesh axis runs over, the one named last changes fastest.
Arguments:
- precision_blocks: bfloat16 [128, 1024, 1024], P('tm', None, 'col'), may hold values from -1 to 1
- coupling: bfloat16 [128, 1024, 1024], P('tm', 'col'), may hold values from -2 to 2
- arrow_rows: bfloat16 [128, 16, 1024], P('tm'), may hold values from -0.1875 to 0.1875
- corner_base: float32 [16, 16], replicated, may hold values from -6 to 6
Outputs:
- sigma_blocks: bfloat16 [128, 1024, 1024], P('tm', None, 'col')
- arrow_block: bfloat16 [128, 16, 1024], P('tm', None, 'col')
- corner: float32 [16, 16], replicated
All inputs are finite; a program needn't handle non-finite values.
Results may differ from a plain program's by a relative error of at most 0.023.
The roundings to bfloat16 on the way count: a program that leaves them out, or rounds other values in their place, can miss the bound.
Values may be sent and summed in bfloat16 or wider, within the bound.
A program may use at most 64 MiB of HBM per device.

v0:
```python
import jax
import jax.numpy as jnp
from jax import lax
from jax.sharding import PartitionSpec as P


def passed_along(array, axis, by):
    count = lax.axis_size(axis)
    pairs = [(i, i + by) for i in range(count) if 0 <= i + by < count]
    return lax.ppermute(array, axis, pairs)


def transposed_dot(left, right):
    return lax.dot_general(
        left, right, (((0,), (0,)), ((), ())), preferred_element_type=jnp.float32
    )


def fold_columns(right_cols, block_piece):
    return jnp.dot(block_piece, right_cols, preferred_element_type=jnp.float32)


def shards(precision_blocks, coupling, arrow_rows, corner_base):
    column_index = lax.axis_index("col")
    panel_width = precision_blocks.shape[2]

    def own_columns(matrix):
        return lax.dynamic_slice_in_dim(matrix, column_index * panel_width, panel_width, 1)

    both_full = lax.all_gather(coupling, "col", axis=1, tiled=True)
    first_full = both_full[0]
    second_full = both_full[1]
    product = fold_columns(
        own_columns(first_full), lax.all_gather(precision_blocks[1], "col", axis=1, tiled=True)
    ).astype(jnp.bfloat16)
    state_s = (
        precision_blocks[0].astype(jnp.float32) + transposed_dot(first_full, product)
    ).astype(jnp.bfloat16)
    full_h = jnp.dot(second_full, first_full, preferred_element_type=jnp.float32).astype(
        jnp.bfloat16
    )
    sections = lax.axis_size("tm").bit_length() - 1
    for section_index in range(sections):
        distance = 1 << section_index
        final_section = section_index + 1 == sections
        if final_section:
            later_s = passed_along(state_s, "tm", -distance)
        else:
            own_rows = lax.dynamic_slice_in_dim(full_h, column_index * panel_width, panel_width, 0)
            later_s, later_h = passed_along((state_s, own_rows), "tm", -distance)
        product = fold_columns(
            own_columns(full_h), lax.all_gather(later_s, "col", axis=1, tiled=True)
        ).astype(jnp.bfloat16)
        new_s = (state_s.astype(jnp.float32) + transposed_dot(full_h, product)).astype(jnp.bfloat16)
        if not final_section:
            new_rows = jnp.dot(later_h, full_h, preferred_element_type=jnp.float32).astype(
                jnp.bfloat16
            )
            full_h = lax.all_gather(new_rows, "col", axis=0, tiled=True)
        state_s = new_s
    next_s = passed_along(state_s, "tm", -1)
    product = fold_columns(
        own_columns(second_full), lax.all_gather(next_s, "col", axis=1, tiled=True)
    ).astype(jnp.bfloat16)
    sigma_odd = (
        precision_blocks[1].astype(jnp.float32) + transposed_dot(second_full, product)
    ).astype(jnp.bfloat16)
    sigma_blocks = jnp.stack([state_s, sigma_odd])
    arrow_full = jnp.einsum(
        "tai,tij->taj", arrow_rows, sigma_blocks, preferred_element_type=jnp.float32
    )
    arrow_cols = lax.dynamic_slice_in_dim(arrow_rows, column_index * panel_width, panel_width, 2)
    corner_term = jnp.einsum("taj,tbj->ab", arrow_full, arrow_cols.astype(jnp.float32))
    time_total = arrow_rows.shape[0] * lax.axis_size("tm")
    corner = corner_base + lax.psum(corner_term, ("tm", "col")) / time_total
    return (sigma_blocks, arrow_full.astype(jnp.bfloat16), corner)


def solution(mesh):
    return jax.shard_map(
        shards,
        mesh=mesh,
        in_specs=(P("tm", None, "col"), P("tm", "col", None), P("tm", None, None), P()),
        out_specs=(P("tm", None, "col"), P("tm", None, "col"), P()),
        check_vma=False,
    )
```

profile of v0, /device:TPU:1, one launch (start us, length us, event | category | flops | bytes accessed | tf_op | source)
XLA Modules:
  0.0 647.5 jit_solution(17266781668212193011)
XLA Ops:
  10.5 53.9 %all-gather.16.cloned.1.call-done = bf16[2,1024,1024]{2,1,0:T(8,128)(2,1)} async-done(((bf16[2,256,1024]{2,1,0:T(8,128)(2,1)}), bf16[2,1024,1024]{2,1,0:T(8,128)(2,1)}) %all-gather.16.cloned.1.call-update) | async-done | bytes 4194320 | tf_op jit(solution)/shard_map/all_gather | solution.py:30
  64.4 4.0 fusion.86
  68.5 31.6 %all-gather.42.cloned.1.call-done = bf16[1,1024,1024]{1,2,0:T(8,128)(2,1)} async-done(((bf16[1,1024,256]{1,2,0:T(8,128)(2,1)}), bf16[1,1024,1024]{1,2,0:T(8,128)(2,1)}) %all-gather.42.cloned.1.call-update) | async-done | bytes 2097168 | tf_op jit(solution)/shard_map/all_gather | solution.py:34
  100.0 3.7 fusion.35
  103.7 2.6 collective-permute-start
  106.3 7.9 %collective-permute-done = bf16[1024,256]{0,1:T(8,128)(2,1)S(1)} collective-permute-done((bf16[1024,256]{0,1:T(8,128)(2,1)S(1)}, bf16[1024,256]{0,1:T(8,128)(2,1)S(1)}, u32[]{:S(2)}, u32[]{:S(2)}) %collective-permute-start) | collective-permute-done | bytes 524320 | tf_op jit(solution)/shard_map/ppermute | solution.py:10
  115.1 4.5 fusion.9
  119.8 2.1 collective-permute-start.1
  121.8 8.6 %collective-permute-done.1 = bf16[256,1024]{1,0:T(8,128)(2,1)S(1)} collective-permute-done((bf16[256,1024]{1,0:T(8,128)(2,1)S(1)}, bf16[256,1024]{1,0:T(8,128)(2,1)S(1)}, u32[]{:S(2)}, u32[]{:S(2)}) %collective-permute-start.1) | collective-permute-done | bytes 524320 | tf_op jit(solution)/shard_map/ppermute | solution.py:10
  130.4 1.5 convolution_convert_fusion.10
  132.0 17.9 %all-gather.18.cloned.1.call-done = bf16[1024,1024]{0,1:T(8,128)(2,1)} async-done(((bf16[1024,256]{0,1:T(8,128)(2,1)}), bf16[1024,1024]{0,1:T(8,128)(2,1)}) %all-gather.18.cloned.1.call-update) | async-done | bytes 2097168 | tf_op jit(solution)/shard_map/all_gather | solution.py:52
  150.0 4.6 fusion.29
  155.9 13.5 %collective-permute-done.2 = bf16[1024,256]{0,1:T(8,128)(2,1)S(1)} collective-permute-done((bf16[1024,256]{0,1:T(8,128)(2,1)S(1)}, bf16[1024,256]{0,1:T(8,128)(2,1)S(1)}, u32[]{:S(2)}, u32[]{:S(2)}) %collective-permute-start.2) | collective-permute-done | bytes 524320 | tf_op jit(solution)/shard_map/ppermute | solution.py:10
  170.2 15.5 %all-gather.20.cloned.1.call-done = bf16[1024,1024]{1,0:T(8,128)(2,1)} async-done(((bf16[256,1024]{1,0:T(8,128)(2,1)}), bf16[1024,1024]{1,0:T(8,128)(2,1)}) %all-gather.20.cloned.1.call-update) | async-done | bytes 2097168 | tf_op jit(solution)/shard_map/all_gather | solution.py:59
  188.0 13.4 %collective-permute-done.3 = bf16[256,1024]{1,0:T(8,128)(2,1)S(1)} collective-permute-done((bf16[256,1024]{1,0:T(8,128)(2,1)S(1)}, bf16[256,1024]{1,0:T(8,128)(2,1)S(1)}, u32[]{:S(2)}, u32[]{:S(2)}) %collective-permute-start.3) | collective-permute-done | bytes 524320 | tf_op jit(solution)/shard_map/ppermute | solution.py:10
  201.4 3.1 convolution_convert_fusion.8
  204.6 16.2 %all-gather.22.cloned.1.call-done = bf16[1024,1024]{0,1:T(8,128)(2,1)} async-done(((bf16[1024,256]{0,1:T(8,128)(2,1)}), bf16[1024,1024]{0,1:T(8,128)(2,1)}) %all-gather.22.cloned.1.call-update) | async-done | bytes 2097168 | tf_op jit(solution)/shard_map/all_gather | solution.py:52
  220.8 5.4 fusion.30
  227.5 15.1 %collective-permute-done.4 = bf16[1024,256]{0,1:T(8,128)(2,1)S(1)} collective-permute-done((bf16[1024,256]{0,1:T(8,128)(2,1)}, bf16[1024,256]{0,1:T(8,128)(2,1)S(1)}, u32[]{:S(2)}, u32[]{:S(2)}) %collective-permute-start.4) | collective-permute-done | bytes 524320 | tf_op jit(solution)/shard_map/ppermute | solution.py:10
  243.5 13.0 %all-gather.24.cloned.1.call-done = bf16[1024,1024]{1,0:T(8,128)(2,1)} async-done(((bf16[256,1024]{1,0:T(8,128)(2,1)}), bf16[1024,1024]{1,0:T(8,128)(2,1)}) %all-gather.24.cloned.1.call-update) | async-done | bytes 2097168 | tf_op jit(solution)/shard_map/all_gather | solution.py:59
  257.6 1.4 collective-permute-start.5
  259.0 14.9 %collective-permute-done.5 = bf16[256,1024]{1,0:T(8,128)(2,1)S(1)} collective-permute-done((bf16[256,1024]{1,0:T(8,128)(2,1)S(1)}, bf16[256,1024]{1,0:T(8,128)(2,1)S(1)}, u32[]{:S(2)}, u32[]{:S(2)}) %collective-permute-start.5) | collective-permute-done | bytes 524320 | tf_op jit(solution)/shard_map/ppermute | solution.py:10
  273.9 3.1 convolution_convert_fusion.6
  277.2 14.5 %all-gather.26.cloned.1.call-done = bf16[1024,1024]{0,1:T(8,128)(2,1)} async-done(((bf16[1024,256]{0,1:T(8,128)(2,1)}), bf16[1024,1024]{0,1:T(8,128)(2,1)}) %all-gather.26.cloned.1.call-update) | async-done | bytes 2097168 | tf_op jit(solution)/shard_map/all_gather | solution.py:52
  291.8 4.6 fusion.31
  297.7 13.5 %collective-permute-done.6 = bf16[1024,256]{0,1:T(8,128)(2,1)S(1)} collective-permute-done((bf16[1024,256]{0,1:T(8,128)(2,1)S(1)}, bf16[1024,256]{0,1:T(8,128)(2,1)S(1)}, u32[]{:S(2)}, u32[]{:S(2)}) %collective-permute-start.6) | collective-permute-done | bytes 524320 | tf_op jit(solution)/shard_map/ppermute | solution.py:10
  312.0 15.6 %all-gather.28.cloned.1.call-done = bf16[1024,1024]{1,0:T(8,128)(2,1)} async-done(((bf16[256,1024]{1,0:T(8,128)(2,1)}), bf16[1024,1024]{1,0:T(8,128)(2,1)}) %all-gather.28.cloned.1.call-update) | async-done | bytes 2097168 | tf_op jit(solution)/shard_map/all_gather | solution.py:59
  330.0 13.4 %collective-permute-done.7 = bf16[256,1024]{1,0:T(8,128)(2,1)S(1)} collective-permute-done((bf16[256,1024]{1,0:T(8,128)(2,1)S(1)}, bf16[256,1024]{1,0:T(8,128)(2,1)S(1)}, u32[]{:S(2)}, u32[]{:S(2)}) %collective-permute-start.7) | collective-permute-done | bytes 524320 | tf_op jit(solution)/shard_map/ppermute | solution.py:10
  343.4 3.1 convolution_convert_fusion.4
  346.5 16.3 %all-gather.30.cloned.1.call-done = bf16[1024,1024]{0,1:T(8,128)(2,1)} async-done(((bf16[1024,256]{0,1:T(8,128)(2,1)}), bf16[1024,1024]{0,1:T(8,128)(2,1)}) %all-gather.30.cloned.1.call-update) | async-done | bytes 2097168 | tf_op jit(solution)/shard_map/all_gather | solution.py:52
  362.9 5.4 fusion.32
  369.5 25.9 %collective-permute-done.8 = bf16[1024,256]{0,1:T(8,128)(2,1)S(1)} collective-permute-done((bf16[1024,256]{0,1:T(8,128)(2,1)}, bf16[1024,256]{0,1:T(8,128)(2,1)S(1)}, u32[]{:S(2)}, u32[]{:S(2)}) %collective-permute-start.8) | collective-permute-done | bytes 524320 | tf_op jit(solution)/shard_map/ppermute | solution.py:10
  396.3 2.2 all-gather.32.cloned.1.call-done
  399.7 1.4 collective-permute-start.9
  401.1 25.7 %collective-permute-done.9 = bf16[256,1024]{1,0:T(8,128)(2,1)S(1)} collective-permute-done((bf16[256,1024]{1,0:T(8,128)(2,1)S(1)}, bf16[256,1024]{1,0:T(8,128)(2,1)S(1)}, u32[]{:S(2)}, u32[]{:S(2)}) %collective-permute-start.9) | collective-permute-done | bytes 524320 | tf_op jit(solution)/shard_map/ppermute | solution.py:10
  426.8 3.1 convolution_convert_fusion.2
  430.0 3.9 all-gather.34.cloned.1.call-done
  433.9 4.6 fusion.33
  439.8 17.3 %collective-permute-done.10 = bf16[1024,256]{0,1:T(8,128)(2,1)S(1)} collective-permute-done((bf16[1024,256]{0,1:T(8,128)(2,1)S(1)}, bf16[1024,256]{0,1:T(8,128)(2,1)S(1)}, u32[]{:S(2)}, u32[]{:S(2)}) %collective-permute-start.10) | collective-permute-done | bytes 524320 | tf_op jit(solution)/shard_map/ppermute | solution.py:10
  457.9 11.6 %all-gather.36.cloned.1.call-done = bf16[1024,1024]{1,0:T(8,128)(2,1)} async-done(((bf16[256,1024]{1,0:T(8,128)(2,1)}), bf16[1024,1024]{1,0:T(8,128)(2,1)}) %all-gather.36.cloned.1.call-update) | async-done | bytes 2097168 | tf_op jit(solution)/shard_map/all_gather | solution.py:59
  469.6 35.3 %all-gather.38.cloned.1.call-done = bf16[1024,1024]{0,1:T(8,128)(2,1)} async-done(((bf16[1024,256]{0,1:T(8,128)(2,1)}), bf16[1024,1024]{0,1:T(8,128)(2,1)}) %all-gather.38.cloned.1.call-update) | async-done | bytes 2097168 | tf_op jit(solution)/shard_map/all_gather | solution.py:52
  504.8 5.5 fusion.34
  510.3 2.6 collective-permute-start.11
  512.9 8.2 %collective-permute-done.11 = bf16[1024,256]{0,1:T(8,128)(2,1)S(1)} collective-permute-done((bf16[1024,256]{0,1:T(8,128)(2,1)}, bf16[1024,256]{0,1:T(8,128)(2,1)S(1)}, u32[]{:S(2)}, u32[]{:S(2)}) %collective-permute-start.11) | collective-permute-done | bytes 524320 | tf_op jit(solution)/shard_map/ppermute | solution.py:10
  521.8 34.8 %all-gather.40.cloned.1.call-done = bf16[1024,1024]{0,1:T(8,128)(2,1)} async-done(((bf16[1024,256]{0,1:T(8,128)(2,1)}), bf16[1024,1024]{0,1:T(8,128)(2,1)}) %all-gather.40.cloned.1.call-update) | async-done | bytes 2097168 | tf_op jit(solution)/shard_map/all_gather | solution.py:63
  556.6 4.8 fusion.41
  563.1 75.9 %psum.7 = f32[16,16]{1,0:T(8,128)S(1)} all-reduce(f32[16,16]{1,0:T(8,128)S(1)} %convolution_bitcast_fusion.1), channel_id=1, replica_groups=mesh['tm'=64,'col'=4] {'tm','col'}, use_global_device_ids=true, to_apply=%region_0.0 | all-reduce | flops 256 | bytes 2048 | tf_op jit(solution)/shard_map/psum | solution.py:75
  639.1 1.3 copy.16
  (83 shorter events, 25.5 us)
Async XLA Ops:
  7.2 555.4 %copy-start = (bf16[2,16,1024]{2,1,0:T(8,128)(2,1)S(1)}, bf16[2,16,1024]{2,1,0:T(8,128)(2,1)}, u32[]{:S(2)}) copy-start(bf16[2,16,1024]{2,1,0:T(8,128)(2,1)} %param.6) | copy-start | bytes 196612
  7.2 57.2 %all-gather.16.cloned.1.call-start = ((), (), s32[]{:S(2)}) async-start(), calls=%async_computation | async-start | bytes 5242880 | tf_op jit(solution)/shard_map/all_gather | solution.py:30
  7.9 92.1 %all-gather.42.cloned.1.call-start = ((), (), s32[]{:S(2)}) async-start(), calls=%async_computation.13 | async-start | bytes 2621440 | tf_op jit(solution)/shard_map/all_gather | solution.py:34
  10.3 139.7 %all-gather.18.cloned.1.call-start = ((), (), s32[]{:S(2)}) async-start(), calls=%async_computation.1 | async-start | bytes 2621440 | tf_op jit(solution)/shard_map/all_gather | solution.py:52
  103.7 16.0 %copy-start.16 = (bf16[1024,256]{0,1:T(8,128)(2,1)}, bf16[1024,256]{0,1:T(8,128)(2,1)S(1)}, u32[]{:S(2)}) copy-start(bf16[1024,256]{0,1:T(8,128)(2,1)S(1)} %fusion.35) | copy-start | bytes 1572868
  103.7 10.5 %collective-permute-start = (bf16[1024,256]{0,1:T(8,128)(2,1)S(1)}, bf16[1024,256]{0,1:T(8,128)(2,1)S(1)}, u32[]{:S(2)}, u32[]{:S(2)}) collective-permute-start(bf16[1024,256]{0,1:T(8,128)(2,1)S(1)} %fusion.35), channel_id=1, source_target_pairs={{4,0},{8,4},{12,8},{16,12},{20,16},{24,20},{28,24},{32,28},{36,32}... | collective-permute-start | bytes 1572872 | tf_op jit(solution)/shard_map/ppermute | solution.py:10
  114.2 0.8 copy-start.6
  115.1 70.6 %all-gather.20.cloned.1.call-start = ((), (), s32[]{:S(2)}) async-start(), calls=%async_computation.2 | async-start | bytes 2621440 | tf_op jit(solution)/shard_map/all_gather | solution.py:59
  119.7 10.7 %copy-start.11 = (bf16[1024,1024]{1,0:T(8,128)(2,1)}, bf16[1024,1024]{1,0:T(8,128)(2,1)S(1)}, u32[]{:S(2)}) copy-start(bf16[1024,1024]{1,0:T(8,128)(2,1)S(1)} %fusion.9) | copy-start | bytes 6291460
  119.8 30.2 %copy-start.17 = (bf16[1024,256]{0,1:T(8,128)(2,1)S(1)}, bf16[1024,256]{0,1:T(8,128)(2,1)}, u32[]{:S(2)}) copy-start(bf16[1024,256]{0,1:T(8,128)(2,1)} %copy-done.16) | copy-start | bytes 1572868
  119.8 10.6 %collective-permute-start.1 = (bf16[256,1024]{1,0:T(8,128)(2,1)S(1)}, bf16[256,1024]{1,0:T(8,128)(2,1)S(1)}, u32[]{:S(2)}, u32[]{:S(2)}) collective-permute-start(bf16[256,1024]{1,0:T(8,128)(2,1)S(1)} %constant_dynamic-slice_fusion.4), channel_id=1, source_target_pairs={{4,0},{8,4},{12,8},{16,12},{20,16},{24,20},{28,24},{32,28},{36,32}... | collective-permute-start | bytes 1572872 | tf_op jit(solution)/shard_map/ppermute | solution.py:10
  132.0 88.8 %all-gather.22.cloned.1.call-start = ((), (), s32[]{:S(2)}) async-start(), calls=%async_computation.3 | async-start | bytes 2621440 | tf_op jit(solution)/shard_map/all_gather | solution.py:52
  154.6 14.8 %collective-permute-start.2 = (bf16[1024,256]{0,1:T(8,128)(2,1)S(1)}, bf16[1024,256]{0,1:T(8,128)(2,1)S(1)}, u32[]{:S(2)}, u32[]{:S(2)}) collective-permute-start(bf16[1024,256]{0,1:T(8,128)(2,1)S(1)} %fusion.29), channel_id=1, source_target_pairs={{8,0},{12,4},{16,8},{20,12},{24,16},{28,20},{32,24},{36,28},{40,32... | collective-permute-start | bytes 1572872 | tf_op jit(solution)/shard_map/ppermute | solution.py:10
  169.4 0.8 copy-start.2
  170.2 86.3 %all-gather.24.cloned.1.call-start = ((), (), s32[]{:S(2)}) async-start(), calls=%async_computation.4 | async-start | bytes 2621440 | tf_op jit(solution)/shard_map/all_gather | solution.py:59
  186.7 14.7 %collective-permute-start.3 = (bf16[256,1024]{1,0:T(8,128)(2,1)S(1)}, bf16[256,1024]{1,0:T(8,128)(2,1)S(1)}, u32[]{:S(2)}, u32[]{:S(2)}) collective-permute-start(bf16[256,1024]{1,0:T(8,128)(2,1)S(1)} %constant_dynamic-slice_fusion.3), channel_id=1, source_target_pairs={{8,0},{12,4},{16,8},{20,12},{24,16},{28,20},{32,24},{36,28},{40,32... | collective-permute-start | bytes 1572872 | tf_op jit(solution)/shard_map/ppermute | solution.py:10
  204.6 87.2 %all-gather.26.cloned.1.call-start = ((), (), s32[]{:S(2)}) async-start(), calls=%async_computation.5 | async-start | bytes 2621440 | tf_op jit(solution)/shard_map/all_gather | solution.py:52
  226.2 16.4 %collective-permute-start.4 = (bf16[1024,256]{0,1:T(8,128)(2,1)}, bf16[1024,256]{0,1:T(8,128)(2,1)S(1)}, u32[]{:S(2)}, u32[]{:S(2)}) collective-permute-start(bf16[1024,256]{0,1:T(8,128)(2,1)} %fusion.30), channel_id=1, source_target_pairs={{16,0},{20,4},{24,8},{28,12},{32,16},{36,20},{40,24},{44,28},{48,3... | collective-permute-start | bytes 1572872 | tf_op jit(solution)/shard_map/ppermute | solution.py:10
  242.6 0.8 copy-start.3
  243.4 84.2 %all-gather.28.cloned.1.call-start = ((), (), s32[]{:S(2)}) async-start(), calls=%async_computation.6 | async-start | bytes 2621440 | tf_op jit(solution)/shard_map/all_gather | solution.py:59
  257.6 34.2 %copy-start.14 = (bf16[1024,256]{0,1:T(8,128)(2,1)S(1)}, bf16[1024,256]{0,1:T(8,128)(2,1)}, u32[]{:S(2)}) copy-start(bf16[1024,256]{0,1:T(8,128)(2,1)} %fusion.30) | copy-start | bytes 1572868
  257.6 16.3 %collective-permute-start.5 = (bf16[256,1024]{1,0:T(8,128)(2,1)S(1)}, bf16[256,1024]{1,0:T(8,128)(2,1)S(1)}, u32[]{:S(2)}, u32[]{:S(2)}) collective-permute-start(bf16[256,1024]{1,0:T(8,128)(2,1)S(1)} %constant_dynamic-slice_fusion.2), channel_id=1, source_target_pairs={{16,0},{20,4},{24,8},{28,12},{32,16},{36,20},{40,24},{44,28},{48,3... | collective-permute-start | bytes 1572872 | tf_op jit(solution)/shard_map/ppermute | solution.py:10
  277.0 85.9 %all-gather.30.cloned.1.call-start = ((), (), s32[]{:S(2)}) async-start(), calls=%async_computation.7 | async-start | bytes 2621440 | tf_op jit(solution)/shard_map/all_gather | solution.py:52
  296.4 14.8 %collective-permute-start.6 = (bf16[1024,256]{0,1:T(8,128)(2,1)S(1)}, bf16[1024,256]{0,1:T(8,128)(2,1)S(1)}, u32[]{:S(2)}, u32[]{:S(2)}) collective-permute-start(bf16[1024,256]{0,1:T(8,128)(2,1)S(1)} %fusion.31), channel_id=1, source_target_pairs={{32,0},{36,4},{40,8},{44,12},{48,16},{52,20},{56,24},{60,28},{64,3... | collective-permute-start | bytes 1572872 | tf_op jit(solution)/shard_map/ppermute | solution.py:10
  311.2 0.8 copy-start.4
  312.0 86.6 %all-gather.32.cloned.1.call-start = ((), (), s32[]{:S(2)}) async-start(), calls=%async_computation.8 | async-start | bytes 2621440 | tf_op jit(solution)/shard_map/all_gather | solution.py:59
  328.7 14.7 %collective-permute-start.7 = (bf16[256,1024]{1,0:T(8,128)(2,1)S(1)}, bf16[256,1024]{1,0:T(8,128)(2,1)S(1)}, u32[]{:S(2)}, u32[]{:S(2)}) collective-permute-start(bf16[256,1024]{1,0:T(8,128)(2,1)S(1)} %constant_dynamic-slice_fusion.1), channel_id=1, source_target_pairs={{32,0},{36,4},{40,8},{44,12},{48,16},{52,20},{56,24},{60,28},{64,3... | collective-permute-start | bytes 1572872 | tf_op jit(solution)/shard_map/ppermute | solution.py:10
  346.5 87.4 %all-gather.34.cloned.1.call-start = ((), (), s32[]{:S(2)}) async-start(), calls=%async_computation.9 | async-start | bytes 2621440 | tf_op jit(solution)/shard_map/all_gather | solution.py:52
  368.3 27.2 %collective-permute-start.8 = (bf16[1024,256]{0,1:T(8,128)(2,1)}, bf16[1024,256]{0,1:T(8,128)(2,1)S(1)}, u32[]{:S(2)}, u32[]{:S(2)}) collective-permute-start(bf16[1024,256]{0,1:T(8,128)(2,1)} %fusion.32), channel_id=1, source_target_pairs={{64,0},{68,4},{72,8},{76,12},{80,16},{84,20},{88,24},{92,28},{96,3... | collective-permute-start | bytes 1572872 | tf_op jit(solution)/shard_map/ppermute | solution.py:10
  395.4 0.8 copy-start.5
  396.3 73.3 %all-gather.36.cloned.1.call-start = ((), (), s32[]{:S(2)}) async-start(), calls=%async_computation.10 | async-start | bytes 2621440 | tf_op jit(solution)/shard_map/all_gather | solution.py:59
  399.7 34.2 %copy-start.15 = (bf16[1024,256]{0,1:T(8,128)(2,1)S(1)}, bf16[1024,256]{0,1:T(8,128)(2,1)}, u32[]{:S(2)}) copy-start(bf16[1024,256]{0,1:T(8,128)(2,1)} %fusion.32) | copy-start | bytes 1572868
  399.7 27.1 %collective-permute-start.9 = (bf16[256,1024]{1,0:T(8,128)(2,1)S(1)}, bf16[256,1024]{1,0:T(8,128)(2,1)S(1)}, u32[]{:S(2)}, u32[]{:S(2)}) collective-permute-start(bf16[256,1024]{1,0:T(8,128)(2,1)S(1)} %constant_dynamic-slice_fusion), channel_id=1, source_target_pairs={{64,0},{68,4},{72,8},{76,12},{80,16},{84,20},{88,24},{92,28},{96,3... | collective-permute-start | bytes 1572872 | tf_op jit(solution)/shard_map/ppermute | solution.py:10
  429.9 74.9 %all-gather.38.cloned.1.call-start = ((), (), s32[]{:S(2)}) async-start(), calls=%async_computation.11 | async-start | bytes 2621440 | tf_op jit(solution)/shard_map/all_gather | solution.py:52
  438.5 18.6 %collective-permute-start.10 = (bf16[1024,256]{0,1:T(8,128)(2,1)S(1)}, bf16[1024,256]{0,1:T(8,128)(2,1)S(1)}, u32[]{:S(2)}, u32[]{:S(2)}) collective-permute-start(bf16[1024,256]{0,1:T(8,128)(2,1)S(1)} %fusion.33), channel_id=1, source_target_pairs={{128,0},{132,4},{136,8},{140,12},{144,16},{148,20},{152,24},{156,2... | collective-permute-start | bytes 1572872 | tf_op jit(solution)/shard_map/ppermute | solution.py:10
  457.0 0.8 copy-start.7
  457.9 98.7 %copy-start.1 = (bf16[1,1024,256]{1,2,0:T(8,128)(2,1)S(1)}, bf16[1,1024,256]{1,2,0:T(8,128)(2,1)}, u32[]{:S(2)}) copy-start(bf16[1,1024,256]{1,2,0:T(8,128)(2,1)} %copy.25) | copy-start | bytes 1572868
  457.9 98.7 %all-gather.40.cloned.1.call-start = ((), (), s32[]{:S(2)}) async-start(), calls=%async_computation.12 | async-start | bytes 2621440 | tf_op jit(solution)/shard_map/all_gather | solution.py:63
  510.3 10.7 %collective-permute-start.11 = (bf16[1024,256]{0,1:T(8,128)(2,1)}, bf16[1024,256]{0,1:T(8,128)(2,1)S(1)}, u32[]{:S(2)}, u32[]{:S(2)}) collective-permute-start(bf16[1024,256]{0,1:T(8,128)(2,1)} %fusion.34), channel_id=1, source_target_pairs={{4,0},{8,4},{12,8},{16,12},{20,16},{24,20},{28,24},{32,28},{36,32}... | collective-permute-start | bytes 1572872 | tf_op jit(solution)/shard_map/ppermute | solution.py:10
  521.0 0.8 copy-start.8
  556.6 4.8 copy-start.9
  561.4 1.2 copy-start.10
  562.6 77.8 %copy-start.13 = (f32[16,16]{1,0:T(8,128)S(1)}, f32[16,16]{1,0:T(8,128)}, u32[]{:S(2)}) copy-start(f32[16,16]{1,0:T(8,128)} %param.7) | copy-start | bytes 3076
  563.0 78.0 %copy-start.12 = (bf16[2,16,256]{2,1,0:T(8,128)(2,1)}, bf16[2,16,256]{2,1,0:T(8,128)(2,1)S(1)}, u32[]{:S(2)}) copy-start(bf16[2,16,256]{2,1,0:T(8,128)(2,1)S(1)} %convolution_bitcast_fusion) | copy-start | bytes 49156
Sparse Core Ops, SparseCore 0:
  9.8 54.5 all-gather.15
  66.2 33.7 all-gather.41
  115.2 34.7 all-gather.17
  152.2 33.4 all-gather.19
  187.3 33.4 all-gather.21
  223.0 33.4 all-gather.23
  258.3 33.4 all-gather.25
  294.1 33.4 all-gather.27
  329.4 33.4 all-gather.29
  365.1 33.4 all-gather.31
  400.4 33.4 all-gather.33
  436.1 33.4 all-gather.35
  471.4 33.4 all-gather.37
  521.9 34.6 all-gather.39
where the time goes:
time: 648 us
  waiting for transfers between devices  460 us (71%)
  blocking collectives  75.9 us (12%)
  matrix products  57.4 us (9%)
  starting transfers between devices  19.8 us (3%)
  local copies, waits for them, and re-layouts  17.9 us (3%)
  between operations  14.2 us (2%)
    ppermute x12, waiting for transfers between devices, passed_along(): return lax.ppermute(array, axis, pairs)  177 us
    all_gather x6, waiting for transfers between devices, shards(): lax.all_gather(later_s, 'col', axis=1, tiled=True)  104 us
    psum x1, blocking collectives, shards(): corner = corner_base + lax.psum(corner_term, ('tm', 'col')) / time_total  75.9 us
    all_gather x5, waiting for transfers between devices, shards(): full_h = lax.all_gather(new_rows, 'col', axis=0, tiled=True)  57.9 us
    all_gather x1, waiting for transfers between devices, shards(): both_full = lax.all_gather(coupling, 'col', axis=1, tiled=True)  53.9 us
    dot_general x8, matrix products, transposed_dot(): lax.dot_general(left, right, (((0,), (0,)), ((), ())), preferred_element_...  38.4 us
    all_gather x1, waiting for transfers between devices, shards(): lax.all_gather(next_s, 'col', axis=1, tiled=True)  34.8 us
    all_gather x1, waiting for transfers between devices, shards(): lax.all_gather(precision_blocks[1], 'col', axis=1, tiled=True)  31.6 us
  transfers between devices with their start and end apart: 26, of which 26 were waited for; matrix products, arithmetic and copies ran while one was open for 8% of the time, Pallas kernels for 0%

commit v1 on v0

v1 whole, which is shorter than its diff:
```python
import functools

import jax
import jax.numpy as jnp
from jax import lax
from jax.experimental import pallas as pl
from jax.experimental.pallas import tpu as pltpu
from jax.sharding import PartitionSpec as P

MESH = pl.DeviceIdType.MESH
BF16 = jnp.bfloat16
F32 = jnp.float32
X = 4
SENDS = 420
RECVS = 420


def dot(a, b):
    return jnp.dot(a, b, preferred_element_type=F32)


class Links:
    def __init__(self, send, recv):
        self.send, self.recv = send, recv
        self.sends = self.recvs = 0
        self.pending = []

    def take_recv(self, count=1):
        base = self.recvs
        self.recvs += count
        assert self.recvs <= RECVS
        return base

    def take_send(self):
        self.sends += 1
        assert self.sends <= SENDS
        return self.sends - 1

    def copy(self, src, dst, slot, tm, col, when=None):
        sem = self.send.at[self.take_send()]

        def start():
            pltpu.make_async_remote_copy(
                src_ref=src, dst_ref=dst, send_sem=sem, recv_sem=self.recv.at[slot],
                device_id=(tm, col), device_id_type=MESH).start()

        def finish():
            pltpu.make_async_copy(src, src, sem).wait()

        if when is None:
            start()
            self.pending.append(finish)
        else:
            pl.when(when)(start)
            self.pending.append(lambda: pl.when(when)(finish))

    def copy_or_keep(self, src, dst, slot, tm, col, here, when=None):
        there = jnp.logical_not(here)
        if when is not None:
            here, there = jnp.logical_and(when, here), jnp.logical_and(when, there)

        @pl.when(here)
        def _():
            pltpu.make_async_copy(src, dst, self.recv.at[slot]).start()

        self.copy(src, dst, slot, tm, col, there)

    def wait(self, dst, slot):
        pltpu.make_async_copy(dst, dst, self.recv.at[slot]).wait()

    def drain(self):
        for finish in self.pending:
            finish()


def kernel(groups, D, G, R, cb, sig, arrow, corner,
           GF, HF, LA, LH, T, PT, A, B, BT, DB, DT, DS, OT, ON, OS, C1, C2, C3, send, recv):
    n, w = D.shape[1], D.shape[2]
    h, hw = n // 2, w // 2
    levels = groups.bit_length() - 1
    gy = min(4, groups)
    gz = groups // gy
    tm, x = lax.axis_index("tm"), lax.axis_index("col")
    i = lax.rem(tm, 2)
    q = tm // 2
    sib = 2 * q + 1 - i
    head = x // 2
    links = Links(send, recv)
    around = [lax.rem(x + d, X) for d in range(X)]
    right, left = around[1], around[3]

    def group_at(offset):
        return lax.rem(q + (offset + groups) % groups, groups)

    partners = [(sib, x)]
    for d in (1, 2, 3):
        partners += [(2 * q + c, around[d]) for c in (0, 1)]
    offsets = set()
    for k in range(levels):
        offsets |= {(1 << k) % groups, (-(1 << k)) % groups}
    partners += [(2 * group_at(o) + i, x) for o in sorted(offsets)]
    qy, qz = lax.rem(q, gy), q // gy
    ys = [(qz * gy + lax.rem(qy + d, gy)) for d in range(1, gy)]
    zs = [(lax.rem(qz + d, gz) * gy + qy) for d in range(1, gz)]
    partners += [(2 * g + i, x) for g in ys + zs]
    barrier = pltpu.get_barrier_semaphore()
    for partner in partners:
        pl.semaphore_signal(barrier, inc=1, device_id=partner, device_id_type=MESH)
    pl.semaphore_wait(barrier, len(partners))

    def rows_of(chip):
        return pl.ds(pl.multiple_of(chip * w, w), w)

    mine = rows_of(x)
    my_half = pl.ds(pl.multiple_of(i * h, h), h)
    its_half = pl.ds(pl.multiple_of((1 - i) * h, h), h)

    def top(chip):
        return pl.ds(pl.multiple_of(chip * w, w), hw)

    def bottom(chip):
        return pl.ds(pl.multiple_of(chip * w + hw, hw), hw)

    class Gather:
        def __init__(self, buf):
            self.buf, self.slot = buf, links.take_recv(6)

        def start(self):
            b, s = self.buf, self.slot
            links.copy(b.at[top(x)], b.at[top(x)], s, tm, right)
            links.copy(b.at[bottom(x)], b.at[bottom(x)], s + 3, tm, left)
            links.copy(b.at[bottom(x)], b.at[bottom(x)], s + 1, tm, right)
            links.copy(b.at[top(x)], b.at[top(x)], s + 2, tm, left)
            return self

        def mid(self):
            b, s = self.buf, self.slot
            links.wait(b.at[top(left)], s)
            links.copy(b.at[top(left)], b.at[top(left)], s + 4, tm, right)
            links.wait(b.at[bottom(right)], s + 3)
            links.copy(b.at[bottom(right)], b.at[bottom(right)], s + 5, tm, left)

        def end(self):
            b, s = self.buf, self.slot
            links.wait(b.at[bottom(left)], s + 1)
            links.wait(b.at[top(right)], s + 2)
            links.wait(b.at[top(around[2])], s + 4)
            links.wait(b.at[bottom(around[2])], s + 5)

    def exchange_start(buf, value):
        slot = links.take_recv()
        buf[i] = value
        links.copy(buf.at[i], buf.at[i], slot, sib, x)
        return lambda: links.wait(buf.at[1 - i], slot)

    class Turn:
        def __init__(self, index):
            self.buf, self.far, self.near = T.at[index], links.take_recv(4), links.take_recv(4)

        def receive(self, own):
            buf = self.buf
            for d in (1, 3, 2):
                s = around[d]
                links.wait(buf.at[s, i], self.far + s)
                links.copy(buf.at[s, i], buf.at[s, i], self.near + s, sib, x)

            @pl.when(jnp.logical_not(own))
            def _():
                links.wait(buf.at[x], self.near + x)

            for d in (1, 3, 2):
                s = around[d]
                links.wait(buf.at[s, 1 - i], self.near + s)

    turns = [0]

    def turn_start(value):
        index = turns[0]
        turns[0] += 1
        turn = Turn(index)
        value = value.astype(BF16)
        own = i == head
        for j in (0, 1):
            PT[index, j] = value[:, j * w:(j + 1) * w].T.reshape(2, hw, w)
        for j in (1, 0):
            chip = 2 * i + j
            for c in (0, 1):
                links.copy(PT.at[index, j, c], turn.buf.at[x, c], turn.far + x,
                           2 * q + c, chip, chip != x)

        @pl.when(own)
        def _():
            turn.buf[x] = PT[index, lax.rem(x, 2)]

        links.copy(PT.at[index, lax.rem(x, 2)], turn.buf.at[x], turn.near + x, sib, x, own)
        return lambda: turn.receive(own)

    def times_halves(L, H):
        return dot(L[0], H[0:h]) + dot(L[1], H[h:n])

    def times_blocks(Tb, H):
        out = dot(Tb[0].reshape(w, w), H[0:w])
        for k in range(1, X):
            out += dot(Tb[k].reshape(w, w), H[k * w:(k + 1) * w])
        return out

    def add_blocks(own, U):
        return jnp.concatenate(
            [own[0].astype(F32) + U[:, :w], own[1].astype(F32) + U[:, w:]], axis=1).astype(BF16)

    def keep_start(stage, buf, value):
        slot = links.take_recv(2)
        for j in (0, 1):
            stage[j] = value[:, j * w:(j + 1) * w].T
        for j in (1, 0):
            links.copy_or_keep(stage.at[j], buf.at[lax.rem(x, 2)], slot + lax.rem(x, 2),
                               2 * q + head, 2 * i + j,
                               jnp.logical_and(2 * i + j == x, head == i))

        def receive():
            for b in (0, 1):
                links.wait(buf.at[b], slot + b)
        return receive

    def spread_start(s, buf, core):
        slot = links.take_recv(2)
        sender = i == core
        for d in (1, 3, 2, 0):
            chip = around[d]
            links.copy_or_keep(D.at[s, rows_of(chip)], buf.at[lax.rem(x, 2)],
                               slot + lax.rem(x, 2), 2 * q + head, chip,
                               jnp.logical_and(d == 0, head == i), sender)

        def receive():
            for b in (0, 1):
                links.wait(buf.at[b], slot + b)
        return receive

    g_near = links.take_recv(2)
    for s in (1 - i, i):
        links.copy(G.at[s, :, its_half], GF.at[2 * i + s, mine], g_near + s, sib, x)

    rows3 = Turn(turns[0])
    turns[0] += 1
    for d in (1, 3, 2):
        chip = around[d]
        for c in (0, 1):
            at = pl.ds(pl.multiple_of(chip * w + c * hw, hw), hw)
            links.copy(D.at[1, at], rows3.buf.at[x, c], rows3.far + x, 2 * q + c, chip, i == 1)
    at = pl.multiple_of(x * w, w)
    DS[...] = D[1, pl.ds(at, w)].reshape(2, hw, w)

    @pl.when(i == 1)
    def _():
        rows3.buf[x] = DS[...]

    links.copy(DS, rows3.buf.at[x], rows3.near + x, sib, x, i == 1)

    for s in (0, 1):
        GF[2 * i + s, mine] = G[s, :, my_half]
    links.wait(GF.at[2 * (1 - i) + i, mine], g_near + i)
    gather2 = Gather(GF.at[2]).start()
    gather1 = Gather(GF.at[1])
    gather0 = Gather(GF.at[0])
    gather3 = Gather(GF.at[3])

    d_near = links.take_recv(2)
    for s in (0, 1):
        OT[s] = D[s, its_half].T
        links.copy(OT.at[s], DT.at[2 * i + s], d_near + s, sib, x)
        DT[2 * i + s] = D[s, my_half].T

    rows3.receive(i == 1)
    got_d1 = spread_start(1, DB.at[0], 0)
    links.wait(GF.at[2 * (1 - i) + 1 - i, mine], g_near + 1 - i)
    x0 = exchange_start(LH.at[0], GF[3, mine])
    gather2.mid()
    gather1.start()
    gather2.end()
    product = times_blocks(rows3.buf, GF.at[2])
    turn = turn_start(product)
    x0()
    x1 = exchange_start(LH.at[1], times_halves(LH.at[0], GF.at[2]).astype(BF16))
    for s in (0, 1):
        links.wait(DT.at[2 * (1 - i) + s], d_near + s)
    gather1.mid()
    turn()
    state = (times_blocks(T.at[1], GF.at[2]) + DT[2].astype(F32)).astype(BF16)
    a1 = exchange_start(LA.at[0], state)
    gather0.start()
    gather1.end()
    x1()
    x2 = exchange_start(LH.at[2], times_halves(LH.at[1], GF.at[1]).astype(BF16))
    a1()
    turn = turn_start(times_halves(LA.at[0], GF.at[1]))
    gather0.mid()
    got_d1()
    turn()
    state = add_blocks(DB.at[0], times_blocks(T.at[2], GF.at[1]))
    a2 = exchange_start(LA.at[1], state)
    gather0.end()
    x2()
    HF[0, mine] = times_halves(LH.at[2], GF.at[0]).astype(BF16)
    a2()
    turn = turn_start(times_halves(LA.at[1], GF.at[0]))
    gather = Gather(HF.at[0]).start()

    def later_start(src, buf, e, keep, want):
        slot, near = links.take_recv(2), links.take_recv(2)
        for c in (0, 1):
            at = pl.ds(c * hw, hw)
            links.copy(src.at[at], buf.at[i, at], slot + c, 2 * group_at(-e) + i, x, keep)

        def receive():
            for c in (0, 1):
                at = pl.ds(c * hw, hw)

                @pl.when(want)
                def _():
                    links.wait(buf.at[i, at], slot + c)

                links.copy(buf.at[i, at], buf.at[i, at], near + c, sib, x, want)

            @pl.when(want)
            def _():
                for c in (0, 1):
                    links.wait(buf.at[1 - i, pl.ds(c * hw, hw)], near + c)

            @pl.when(jnp.logical_not(want))
            def _():
                buf[...] = jnp.zeros_like(buf)
        return receive

    def send_state(src, buf, e):
        return later_start(src, buf, e, q >= e, q + e < groups)

    def send_map(src, buf, e):
        return later_start(src, buf, e, jnp.logical_and(q >= e, q + e < groups),
                           q + 2 * e < groups)

    got_h = send_map(HF.at[0, mine], LH.at[3], 1) if levels > 1 else None
    gather.mid()
    turn()
    A[0] = (times_blocks(T.at[3], GF.at[0]) + DT[0].astype(F32)).astype(BF16)
    got_a = send_state(A.at[0], LA.at[2], 1)
    got_b = keep_start(BT.at[0], B.at[0], A[0])
    got_d2 = None
    for k in range(levels):
        final = k + 1 == levels
        e = 1 << k
        gather.end()
        if not final:
            got_h()
            HF[k + 1, mine] = times_halves(LH.at[3 + k], HF.at[k]).astype(BF16)
            gather = Gather(HF.at[k + 1]).start()
            if k + 2 < levels:
                got_h = send_map(HF.at[k + 1, mine], LH.at[4 + k], 2 * e)
        else:
            gather3.start()
            gather = gather3
            got_d2 = spread_start(0, DB.at[1], 1)
        got_a()
        turn = turn_start(times_halves(LA.at[2 + k], HF.at[k]))
        gather.mid()
        got_b()
        turn()
        A[k + 1] = add_blocks(B.at[k], times_blocks(T.at[4 + k], HF.at[k]))
        if not final:
            got_a = send_state(A.at[k + 1], LA.at[3 + k], 2 * e)
            got_b = keep_start(BT.at[k + 1], B.at[k + 1], A[k + 1])

    def out_rows_start(index, value, core):
        slot = links.take_recv(X)
        for j in (0, 1):
            ON[index, j] = value[:, j * w:(j + 1) * w]
        for j in (1, 0):
            chip = 2 * i + j
            links.copy_or_keep(ON.at[index, j], sig.at[0, mine], slot + x, 2 * q + core, chip,
                               jnp.logical_and(chip == x, i == core))

        def receive():
            @pl.when(i == core)
            def _():
                for chip in range(X):
                    links.wait(sig.at[0, pl.ds(chip * w, w)], slot + chip)
        return receive

    def out_turned_start(index, value, core):
        slot = links.take_recv(2)
        OS[index] = value.T
        links.copy_or_keep(OS.at[index], sig.at[1, my_half], slot + i, 2 * q + core, x, i == core)

        def receive():
            @pl.when(i == core)
            def _():
                for c in (0, 1):
                    links.wait(sig.at[1, pl.ds(c * h, h)], slot + c)
        return receive

    base = 2 + levels
    got_a = send_state(A.at[levels], LA.at[base], 1)
    out0 = out_rows_start(0, A[levels], 0)
    gather3.end()
    got_a()
    turn = turn_start(times_halves(LA.at[base], GF.at[3]))
    turn()
    state = (times_blocks(T.at[4 + levels], GF.at[3]) + DT[3].astype(F32)).astype(BF16)
    a3 = exchange_start(LA.at[base + 1], state)
    out3 = out_turned_start(0, state, 1)
    a3()
    turn = turn_start(times_halves(LA.at[base + 1], GF.at[2]))
    got_d2()
    turn()
    state = add_blocks(DB.at[1], times_blocks(T.at[5 + levels], GF.at[2]))
    a4 = exchange_start(LA.at[base + 2], state)
    out2 = out_rows_start(1, state, 1)
    a4()
    turn = turn_start(times_halves(LA.at[base + 2], GF.at[1]))
    out0()
    out3()
    out2()
    turn()
    state = (times_blocks(T.at[6 + levels], GF.at[1]) + DT[1].astype(F32)).astype(BF16)
    out1 = out_turned_start(1, state, 0)

    out1()
    total = jnp.zeros((R.shape[1], R.shape[1]), F32)
    for s in (0, 1):
        full = dot(R[s], sig[s])
        arrow[s] = full.astype(BF16)
        panel = R[s, :, pl.ds(pl.multiple_of(x * w, w), w)].astype(F32)
        total += lax.dot_general(full, panel, (((1,), (1,)), ((), ())),
                                 precision=lax.Precision.HIGHEST, preferred_element_type=F32)

    def share(buf, place, others):
        slot = links.take_recv(buf.shape[0])
        for device in others:
            links.copy(buf.at[place], buf.at[place], slot + place, *device)
        for d in range(1, buf.shape[0]):
            at = lax.rem(place + d, buf.shape[0])
            links.wait(buf.at[at], slot + at)
        out = buf[0]
        for k in range(1, buf.shape[0]):
            out += buf[k]
        return out

    ar = R.shape[1]
    C1[2 * x + i] = jnp.concatenate([total, jnp.zeros((ar, C1.shape[2] - ar), F32)], axis=1)
    total = share(C1, 2 * x + i, [(sib, x)] + [(2 * q + c, around[d]) for d in (1, 2, 3)
                                                for c in (0, 1)])
    if gy > 1:
        C2[qy] = total
        total = share(C2, qy, [(2 * g + i, x) for g in ys])
    if gz > 1:
        C3[qz] = total
        total = share(C3, qz, [(2 * g + i, x) for g in zs])
    corner[...] = cb[...] + total[:, :ar] / (4 * groups)
    links.drain()


def shards(precision_blocks, coupling, arrow_rows, corner_base):
    groups = lax.axis_size("tm") // 2
    levels = groups.bit_length() - 1
    n, w = precision_blocks.shape[1:]
    ar = arrow_rows.shape[1]
    h, hw = n // 2, w // 2
    vmem = pl.BlockSpec(memory_space=pltpu.VMEM)
    return pl.pallas_call(
        functools.partial(kernel, groups),
        out_shape=(
            jax.ShapeDtypeStruct(precision_blocks.shape, BF16),
            jax.ShapeDtypeStruct((2, ar, w), BF16),
            jax.ShapeDtypeStruct((ar, ar), F32),
        ),
        in_specs=[vmem] * 4,
        out_specs=(vmem,) * 3,
        scratch_shapes=[
            pltpu.VMEM((4, n, h), BF16),
            pltpu.VMEM((levels, n, h), BF16),
            pltpu.VMEM((levels + 5, 2, w, h), BF16),
            pltpu.VMEM((levels + 2, 2, w, h), BF16),
            pltpu.VMEM((levels + 7, X, 2, hw, w), BF16),
            pltpu.VMEM((levels + 7, 2, 2, hw, w), BF16),
            pltpu.VMEM((levels + 1, w, h), BF16),
            pltpu.VMEM((levels, 2, w, w), BF16),
            pltpu.VMEM((levels, 2, w, w), BF16),
            pltpu.VMEM((2, 2, w, w), BF16),
            pltpu.VMEM((4, w, h), BF16),
            pltpu.VMEM((2, hw, w), BF16),
            pltpu.VMEM((2, w, h), BF16),
            pltpu.VMEM((2, 2, w, w), BF16),
            pltpu.VMEM((2, h, w), BF16),
            pltpu.VMEM((8, ar, 128), F32),
            pltpu.VMEM((min(4, groups), ar, 128), F32),
            pltpu.VMEM((max(1, groups // 4), ar, 128), F32),
            pltpu.SemaphoreType.DMA((SENDS,)),
            pltpu.SemaphoreType.DMA((RECVS,)),
        ],
        compiler_params=pltpu.CompilerParams(
            collective_id=0, has_side_effects=True, vmem_limit_bytes=60 * 1024 * 1024),
        cost_estimate=pl.CostEstimate(
            flops=2 * 22 * w * n * n, bytes_accessed=4 << 20, transcendentals=0),
    )(precision_blocks, coupling, arrow_rows, corner_base)


def solution(mesh):
    return jax.shard_map(
        shards,
        mesh=mesh,
        in_specs=(P("tm", None, "col"), P("tm", "col", None), P("tm", None, None), P()),
        out_specs=(P("tm", None, "col"), P("tm", None, "col"), P()),
        check_vma=False,
    )
```

time: 648 us -> 218 us (0.34)
  waiting for transfers between devices: 460 us -> 0 us
  Pallas kernels: 0 us -> 214 us
  blocking collectives: 75.9 us -> 0 us
  matrix products: 57.4 us -> 0 us
  starting transfers between devices: 19.8 us -> 0 us
  local copies, waits for them, and re-layouts: 17.9 us -> 3.57 us
  between operations: 14.2 us -> 0.65 us
    all_gather x14 -> x0, waiting for transfers between devices: 282 us -> none  [the longest x6 104 us: shards(): lax.all_gather(later_s, 'col', axis=1, tiled=True)]
    pallas_call x0 -> x1, Pallas kernels: none -> 214 us  [shards(): pl.pallas_call(functools.partial(kernel, groups), out_shape=(jax.ShapeDty...]
    ppermute x12 -> x0, waiting for transfers between devices: 177 us -> none  [passed_along(): return lax.ppermute(array, axis, pairs)]
    psum x1 -> x0, blocking collectives: 75.9 us -> none  [shards(): corner = corner_base + lax.psum(corner_term, ('tm', 'col')) / time_total]
    dot_general x16 -> x0, matrix products: 57.4 us -> none  [the longest x8 38.4 us: transposed_dot(): lax.dot_general(left, right, (((0,), (0,)), ((), ())), preferred_element_...]
    ppermute x12 -> x0, starting transfers between devices: 19.1 us -> none  [passed_along(): return lax.ppermute(array, axis, pairs)]
  transfers between devices with their start and end apart: 26 -> 0, of which waited for: 26 -> 0; matrix products, arithmetic and copies ran while one was open for 8% -> 0% of each run, Pallas kernels for 0% -> 0%
where the time goes in v1:
time: 218 us
  Pallas kernels  214 us (98%)
  local copies, waits for them, and re-layouts  3.57 us (2%)
    pallas_call x1, Pallas kernels, shards(): pl.pallas_call(functools.partial(kernel, groups), out_shape=(jax.ShapeDty...  214 us

profile of v1, /device:TPU:1, one launch (start us, length us, event | category | flops | bytes accessed | tf_op | source)
XLA Modules:
  0.0 217.8 jit_solution(11761473839144037219)
XLA Ops:
  0.6 213.6 %shard_map.67 = (bf16[2,1024,256]{2,1,0:T(8,128)(2,1)}, bf16[2,16,256]{2,1,0:T(8,128)(2,1)}, f32[16,16]{1,0:T(8,128)}) custom-call(bf16[2,1024,256]{2,1,0:T(8,128)(2,1)} %D.1, bf16[2,256,1024]{2,1,0:T(8,128)(2,1)} %G.1, bf16[2,16,1024]{2,1,0:T(8,128)(2,1)} %R.1, f32[16,16]{1,0:T(8,128)} %cb.1), custom_call_target="tpu_custom_call" | custom-call | flops 11811160064 | bytes 4194304 | tf_op jit(solution)/shard_map/pallas_call | solution.py:468
  214.2 0.0 copy-start
  214.2 2.3 %copy.10 = bf16[2,1024,256]{2,1,0:T(8,128)(2,1)} copy(bf16[2,1024,256]{2,1,0:T(8,128)(2,1)} %get-tuple-element.6) | data formatting | bytes 2097152
  216.5 0.0 copy-done
  216.5 0.0 copy-start.1
  216.5 0.6 copy.11
  217.1 0.1 copy-done.1
  217.2 0.6 copy.12
Async XLA Ops:
  214.2 2.3 %copy-start = (bf16[2,16,256]{2,1,0:T(8,128)(2,1)S(1)}, bf16[2,16,256]{2,1,0:T(8,128)(2,1)}, u32[]{:S(2)}) copy-start(bf16[2,16,256]{2,1,0:T(8,128)(2,1)} %get-tuple-element.7) | copy-start | bytes 49156
  216.5 0.7 copy-start.1

commit v2 on v0

v2 whole, which is shorter than its diff:
```python
import functools

import jax
import jax.numpy as jnp
from jax import lax
from jax.experimental import pallas as pl
from jax.experimental.pallas import tpu as pltpu
from jax.sharding import PartitionSpec as P

MESH = pl.DeviceIdType.MESH
BF16 = jnp.bfloat16
F32 = jnp.float32
X = 4
CHUNKS = 2
SEMS = 190


def dot(a, b):
    return jnp.dot(a, b, preferred_element_type=F32)


class Links:
    def __init__(self, sems):
        self.sems, self.used, self.pending = sems, 0, []

    def take(self, count=1):
        base = self.used
        self.used += count
        assert self.used <= SEMS
        return base

    def copy(self, src, dst, sent, got, tm, col, when=None):
        def start():
            pltpu.make_async_remote_copy(
                src_ref=src, dst_ref=dst, send_sem=self.sems.at[sent], recv_sem=self.sems.at[got],
                device_id=(tm, col), device_id_type=MESH).start()

        start() if when is None else pl.when(when)(start)

    def keep(self, src, dst, got, when=None):
        def start():
            pltpu.make_async_copy(src, dst, self.sems.at[got]).start()

        start() if when is None else pl.when(when)(start)

    def wait(self, ref, sem, when=None):
        def finish():
            pltpu.make_async_copy(ref, ref, self.sems.at[sem]).wait()

        finish() if when is None else pl.when(when)(finish)

    def later(self, ref, sem, when=None):
        self.pending.append((ref, sem, when))

    def drain(self):
        for ref, sem, when in self.pending:
            self.wait(ref, sem, when)


def kernel(groups, D, G, R, cb, sig, arrow, corner,
           GF, HA, HB, HC, HF, A, LA, LH, PS, PC, DC, DR, SB, RR, OT, C1, C2, C3, sems):
    n, w = D.shape[1], D.shape[2]
    h = n // 2
    m = w // 2
    hm = m // 2
    cm = m // CHUNKS
    levels = groups.bit_length() - 1
    gy = min(4, groups)
    gz = groups // gy
    tm, x = lax.axis_index("tm"), lax.axis_index("col")
    i = lax.rem(tm, 2)
    q = tm // 2
    sib = 2 * q + 1 - i
    me = 2 * x + i
    links = Links(sems)
    around = [lax.rem(x + d, X) for d in range(X)]
    right, left = around[1], around[3]
    ring = [(around[d], c) for d in (1, 3, 2) for c in (0, 1)]
    qy, qz = lax.rem(q, gy), q // gy
    ys = [(qz * gy + lax.rem(qy + d, gy)) for d in range(1, gy)]
    zs = [(lax.rem(qz + d, gz) * gy + qy) for d in range(1, gz)]

    def group_at(offset):
        return lax.rem(q + (offset + groups) % groups, groups)

    partners = [(sib, x)] + [(2 * q + c, chip) for chip, c in ring]
    offsets = set()
    for k in range(levels):
        offsets |= {(1 << k) % groups, (-(1 << k)) % groups}
    partners += [(2 * group_at(o) + i, x) for o in sorted(offsets)]
    partners += [(2 * g + i, x) for g in ys + zs]
    barrier = pltpu.get_barrier_semaphore()
    for partner in partners:
        pl.semaphore_signal(barrier, inc=1, device_id=partner, device_id_type=MESH)

    def rows(place, size=m, part=0):
        return pl.ds(pl.multiple_of(place * m + part * size, size), size)

    def panel(chip):
        return pl.ds(pl.multiple_of(chip * w, w), w)

    mine = rows(me)
    my_lanes = pl.ds(pl.multiple_of(i * m, m), m)
    its_lanes = pl.ds(pl.multiple_of((1 - i) * m, m), m)

    pair, its_pair = pl.ds(2 * i, 2), pl.ds(2 * (1 - i), 2)
    g_here, d_here, r_here = links.take(2), links.take(), links.take()
    for s in (0, 1):
        links.keep(G.at[s], GF.at[2 * i + s, panel(x)], g_here + s)
    for s in (0, 1):
        links.keep(D.at[s, :, my_lanes], DC.at[2 * i + s], d_here)
        links.keep(R.at[s], RR.at[2 * i + s], r_here)
    pl.semaphore_wait(barrier, len(partners))
    g_sent, g_near = links.take(), links.take(2)
    d_sent, d_near = links.take(), links.take()
    r_sent, r_near = links.take(), links.take()
    links.copy(G.at[0], GF.at[2 * i, panel(x)], g_sent, g_near, sib, x)
    links.copy(D.at[1, :, its_lanes], DC.at[2 * i + 1], d_sent, d_near, sib, x)
    links.copy(G.at[1], GF.at[2 * i + 1, panel(x)], g_sent, g_near + 1, sib, x)
    links.copy(D.at[0, :, its_lanes], DC.at[2 * i], d_sent, d_near, sib, x)
    for s in (0, 1):
        links.copy(R.at[s], RR.at[2 * i + s], r_sent, r_near, sib, x)
    links.later(GF.at[pair, panel(x)], g_sent)
    links.later(DC.at[pair], d_sent)
    links.later(RR.at[pair], r_sent)

    class Gather:
        def __init__(self, buf, own=True):
            self.buf, self.own = buf, own
            self.sent, self.got, self.near = links.take(), links.take(4), links.take()
            links.later(buf.at[pl.ds(0, (7 if own else 6) * m)], self.sent)

        def piece(self, chip, core, half):
            return self.buf.at[rows(2 * chip + core, hm, half)]

        def pass_on(self, ref, slot, chip):
            links.copy(ref, ref, self.sent, self.got + slot, tm, chip)

        def share(self, ref):
            links.copy(ref, ref, self.sent, self.near, sib, x)

        def start(self):
            top, bottom = self.piece(x, i, 0), self.piece(x, i, 1)
            self.pass_on(top, 0, right)
            self.pass_on(bottom, 1, left)
            self.pass_on(bottom, 2, right)
            self.pass_on(top, 2, left)
            if self.own:
                self.share(self.buf.at[mine])
            return self

        def mid(self):
            for ref, slot, chip in ((self.piece(left, i, 0), 0, right),
                                    (self.piece(right, i, 1), 1, left)):
                links.wait(ref, self.got + slot)
                self.pass_on(ref, 3, chip)
                self.share(ref)

        def end(self):
            opposite = around[2]
            for slot, refs in ((2, (self.piece(left, i, 1), self.piece(right, i, 0))),
                               (3, (self.piece(opposite, i, 0), self.piece(opposite, i, 1)))):
                links.wait(self.buf.at[mine], self.got + slot)
                for ref in refs:
                    self.share(ref)
            links.wait(self.buf.at[pl.ds(0, (4 if self.own else 3) * m)], self.near)

    class Turn:
        def __init__(self, stage, buf, parts):
            self.stage, self.buf, self.parts = stage, buf, parts
            self.sent, self.got = links.take(), links.take()
            links.later(stage.at[pl.ds(0, 2 * X - 1)], self.sent)

        def send(self, part, value):
            size = m // self.parts
            at = pl.ds(part * size, size)
            value = value.astype(BF16)
            for b in range(2 * X):
                self.stage[b, at] = value[:, b * m:(b + 1) * m]
            to = pl.ds(pl.multiple_of(me * m + part * size, size), size)
            for chip, c in ring:
                links.copy(self.stage.at[2 * chip + c, at], self.buf.at[to], self.sent, self.got,
                           2 * q + c, chip)
            links.copy(self.stage.at[2 * x + 1 - i, at], self.buf.at[to], self.sent, self.got,
                       sib, x)
            self.buf[to] = self.stage[me, at]

        def receive(self):
            links.wait(self.buf.at[pl.ds(0, (2 * X - 1) * m)], self.got)

        def turned(self):
            return self.buf[...].T

    turns = [0]

    def new_turn(parts=1):
        turns[0] += 1
        return Turn(PS.at[turns[0] - 1], PC.at[turns[0] - 1], parts)

    def turn_of(value):
        turn = new_turn()
        turn.send(0, value)
        return turn

    class Rows:
        def __init__(self, s, core, buf):
            self.s, self.sender, self.buf = s, i == core, buf
            self.sent, self.got = links.take(), links.take()

        def start(self):
            to = self.buf.at[:, panel(x)]
            for chip, c in ring + [(x, 1 - i)]:
                links.copy(D.at[self.s, rows(2 * chip + c)], to, self.sent, self.got,
                           2 * q + c, chip, self.sender)
            links.keep(D.at[self.s, mine], to, self.got, self.sender)
            links.later(D.at[self.s, pl.ds(0, (2 * X - 1) * m)], self.sent, self.sender)
            return self

        def receive(self):
            links.wait(self.buf, self.got)

    def column(t):
        return DC[t].T.astype(F32)

    def whole_product(out, L, H):
        sent, got = links.take(), links.take()
        for j in range(4):
            at = rows(4 * i + j)
            out[at] = dot(L[at], H[...]).astype(BF16)
            links.copy(out.at[at], out.at[at], sent, got, sib, x)
        links.later(out.at[pl.ds(pl.multiple_of(i * h, h), h)], sent)
        return lambda: links.wait(out.at[pl.ds(pl.multiple_of((1 - i) * h, h), h)], got)

    first0 = i == 0
    links.wait(GF.at[2 * i, panel(x)], g_here)
    links.wait(GF.at[2, panel(x)], g_near, first0)
    gather2 = Gather(GF.at[2], False).start()
    links.wait(GF.at[0, panel(x)], g_near, jnp.logical_not(first0))
    gather2.mid()
    gather0 = Gather(GF.at[0], False).start()
    rows2 = Rows(0, 1, DR.at[1]).start()
    links.wait(GF.at[2 * i + 1, panel(x)], g_here + 1)
    links.wait(GF.at[2 * (1 - i) + 1, panel(x)], g_near + 1)
    links.wait(DC.at[pair], d_here)
    links.wait(RR.at[pair], r_here)
    links.wait(DC.at[its_pair], d_near)
    links.wait(RR.at[its_pair], r_near)
    gather2.end()
    turn_b = turn_of(dot(DC[3].T, GF[2]))
    Hb = dot(GF[3, mine], GF[2]).astype(BF16)
    gather0.mid()
    gather1 = Gather(GF.at[1], False).start()
    gather0.end()
    rows2.receive()
    turn_b.receive()
    SB[0] = (DR[1].astype(F32) + dot(turn_b.turned(), GF[2])).astype(BF16)
    gather1.mid()
    rows1 = Rows(1, 0, DR.at[0]).start()
    gather1.end()
    got_ha = whole_product(HA, GF.at[1], GF.at[0])
    rows1.receive()
    turn_a = turn_of(dot(DR[0], GF[0]))
    got_ha()
    turn = turn_of(dot(SB[0], HA[...]))
    HF[0, mine] = dot(Hb, HA[...]).astype(BF16)
    gather = Gather(HF.at[0]).start()
    turn_a.receive()
    Sa = (column(0) + dot(turn_a.turned(), GF[0])).astype(BF16)

    def later_start(src, buf, e, keep, want, parts):
        sent, got, size = links.take(), links.take(parts), m // parts
        for c in range(parts):
            at = pl.ds(c * size, size)
            links.copy(src.at[at], buf.at[at], sent, got + c, 2 * group_at(-e) + i, x, keep)
        links.later(src, sent, keep)

        @pl.when(jnp.logical_not(want))
        def _():
            buf[...] = jnp.zeros_like(buf)

        return lambda c: links.wait(buf.at[pl.ds(c * size, size)], got + c, want)

    def send_state(src, buf, e):
        return later_start(src, buf, e, q >= e, q + e < groups, CHUNKS)

    def send_map(src, buf, e):
        return later_start(src, buf, e, jnp.logical_and(q >= e, q + e < groups),
                           q + 2 * e < groups, 1)

    def apply_later(got, L, H):
        turn = new_turn(CHUNKS)
        for c in range(CHUNKS):
            got(c)
            turn.send(c, dot(L[pl.ds(c * cm, cm)], H[...]))
        return turn

    got_h = send_map(HF.at[0, mine], LH.at[0], 1) if levels > 1 else None
    gather.mid()
    turn.receive()
    A[0] = (Sa.astype(F32) + dot(turn.turned(), HA[...])).astype(BF16)
    got_a = send_state(A.at[0], LA.at[0], 1)
    own = turn_of(A[0])
    for k in range(levels):
        final = k + 1 == levels
        e = 1 << k
        gather.end()
        if not final:
            got_h(0)
            HF[k + 1, mine] = dot(LH[k], HF[k]).astype(BF16)
            gather = Gather(HF.at[k + 1]).start()
            if k + 2 < levels:
                got_h = send_map(HF.at[k + 1, mine], LH.at[k + 1], 2 * e)
        else:
            gather = gather3 = Gather(GF.at[3], False).start()
            gather3.mid()
        turn = apply_later(got_a, LA.at[k], HF.at[k])
        if final:
            turn_c = turn_of(dot(SB[0], GF[1]))
            turn_s = turn_of(SB[0])
        else:
            gather.mid()
        own.receive()
        before = own.turned().astype(F32)
        turn.receive()
        A[k + 1] = (before + dot(turn.turned(), HF[k])).astype(BF16)
        got_a = send_state(A.at[k + 1], LA.at[k + 1], 1 if final else 2 * e)
        if not final:
            own = turn_of(A[k + 1])

    class RowsOut:
        def __init__(self, src, core, s):
            self.core, self.s, self.got = core, s, links.take()
            to, sent, near = sig.at[s, mine], links.take(), links.take()
            for d in (1, 3, 2):
                links.copy(src.at[:, panel(around[d])], to, sent, self.got, 2 * q + core, around[d])
            links.copy(src.at[:, panel(x)], to, near, self.got, sib, x, i != core)
            links.keep(src.at[:, panel(x)], to, self.got, i == core)
            links.later(src.at[:, pl.ds(0, 3 * w)], sent)
            links.later(src.at[:, panel(x)], near, i != core)

        def receive(self):
            links.wait(sig.at[self.s], self.got, i == self.core)

    class ColumnsOut:
        def __init__(self, stage, value, core, s):
            self.core, self.s, self.got, sent = core, s, links.take(), links.take()
            stage[...] = value.T
            links.copy(stage, sig.at[s, :, my_lanes], sent, self.got, sib, x, i != core)
            links.later(stage, sent, i != core)

            @pl.when(i == core)
            def _():
                sig[s, :, my_lanes] = stage[...]

        def receive(self):
            links.wait(sig.at[self.s, :, its_lanes], self.got, i == self.core)

    class Sum:
        def __init__(self, buf, place, value, others):
            size = buf.shape[0]
            self.buf, self.others, sent, self.got = (
                buf, buf.at[pl.ds(0, size - 1)], links.take(), links.take())
            buf[place] = value
            for device in others:
                links.copy(buf.at[place], buf.at[place], sent, self.got, *device)
            links.later(self.others, sent)

        def receive(self):
            links.wait(self.others, self.got)
            out = self.buf[0]
            for k in range(1, self.buf.shape[0]):
                out += self.buf[k]
            return out

    def small(a, b, dims):
        return lax.dot_general(a, b, (dims, ((), ())), precision=lax.Precision.HIGHEST,
                               preferred_element_type=F32)

    def by_lanes(a, b):
        return lax.dot_general(a, b, (((1,), (1,)), ((), ())), preferred_element_type=F32)

    out0 = RowsOut(A.at[levels], 0, 0)
    gather3.end()
    got_hb = whole_product(HB, GF.at[3], GF.at[2])
    got_hb()
    got_hc = whole_product(HC, HB, GF.at[1])
    turn_c.receive()
    SB[1] = (column(1) + dot(turn_c.turned(), GF[1])).astype(BF16)
    turn_s.receive()
    own_terms = {3: DC[3].T, 2: turn_s.turned(), 1: SB[1]}
    maps = {3: GF.at[3], 2: HB, 1: HC}
    ar = R.shape[1]
    my_arrow = [RR[t, :, pl.ds(pl.multiple_of(me * m, m), m)].astype(F32) for t in range(4)]
    total = small(my_arrow[0], by_lanes(A[levels], RR[0]), ((1,), (0,)))
    for t in (1, 2, 3):
        total += small(by_lanes(own_terms[t], RR[t]), my_arrow[t], ((0,), (1,)))
    got_hc()
    V = {t: by_lanes(RR[t], maps[t][mine]) for t in (1, 2, 3)}
    turns_out = {t: new_turn(CHUNKS) for t in (3, 2, 1)}
    products = []
    for c in range(CHUNKS):
        got_a(c)
        for t in (3, 2, 1):
            product = dot(LA[levels, pl.ds(c * cm, cm)], maps[t][...]).astype(BF16)
            turns_out[t].send(c, product)
            products.append((t, c, product))
    for t, c, product in products:
        total += small(V[t][:, c * cm:(c + 1) * cm], by_lanes(product, RR[t]), ((1,), (0,)))
    total = jnp.concatenate([total, jnp.zeros((ar, C1.shape[2] - ar), F32)], axis=1)
    total = Sum(C1, me, total, [(sib, x)] + [(2 * q + c, chip) for chip, c in ring]).receive()
    if gy > 1:
        total = Sum(C2, qy, total, [(2 * g + i, x) for g in ys]).receive()
    if gz > 1:
        corner_sum = Sum(C3, qz, total, [(2 * g + i, x) for g in zs])

    def sigma_of(t):
        turns_out[t].receive()
        value = (own_terms[t].astype(F32) + dot(turns_out[t].turned(), maps[t][...])).astype(BF16)
        return ColumnsOut(OT.at[t - 1], value, t // 2, t % 2)

    outs = [out0, sigma_of(3), sigma_of(2), sigma_of(1)]
    for out in outs:
        out.receive()
    for s in (0, 1):
        arrow[s] = dot(RR[2 * i + s], sig[s]).astype(BF16)
    if gz > 1:
        total = corner_sum.receive()
    corner[...] = cb[...] + total[:, :ar] / (4 * groups)
    links.drain()


def shards(precision_blocks, coupling, arrow_rows, corner_base):
    groups = lax.axis_size("tm") // 2
    levels = groups.bit_length() - 1
    assert levels % 2 == 1
    n, w = precision_blocks.shape[1:]
    ar = arrow_rows.shape[1]
    m = w // 2
    vmem = pl.BlockSpec(memory_space=pltpu.VMEM)
    far = pl.BlockSpec(memory_space=pl.ANY)
    turns = 2 * levels + 8
    return pl.pallas_call(
        functools.partial(kernel, groups),
        out_shape=(
            jax.ShapeDtypeStruct(precision_blocks.shape, BF16),
            jax.ShapeDtypeStruct((2, ar, w), BF16),
            jax.ShapeDtypeStruct((ar, ar), F32),
        ),
        in_specs=[far, far, far, vmem],
        out_specs=(vmem,) * 3,
        scratch_shapes=[
            pltpu.VMEM((4, n, n), BF16),
            pltpu.VMEM((n, n), BF16),
            pltpu.VMEM((n, n), BF16),
            pltpu.VMEM((n, n), BF16),
            pltpu.VMEM((levels, n, n), BF16),
            pltpu.VMEM((levels + 1, m, n), BF16),
            pltpu.VMEM((levels + 1, m, n), BF16),
            pltpu.VMEM((levels, m, n), BF16),
            pltpu.VMEM((turns, 2 * X, m, m), BF16),
            pltpu.VMEM((turns, n, m), BF16),
            pltpu.VMEM((4, n, m), BF16),
            pltpu.VMEM((2, m, n), BF16),
            pltpu.VMEM((2, m, n), BF16),
            pltpu.VMEM((4, ar, n), BF16),
            pltpu.VMEM((3, n, m), BF16),
            pltpu.VMEM((8, ar, 128), F32),
            pltpu.VMEM((min(4, groups), ar, 128), F32),
            pltpu.VMEM((max(1, groups // 4), ar, 128), F32),
            pltpu.SemaphoreType.DMA((SEMS,)),
        ],
        compiler_params=pltpu.CompilerParams(
            collective_id=0, has_side_effects=True, vmem_limit_bytes=60 * 1024 * 1024),
        cost_estimate=pl.CostEstimate(
            flops=2 * 22 * w * n * n, bytes_accessed=4 << 20, transcendentals=0),
    )(precision_blocks, coupling, arrow_rows, corner_base)


def solution(mesh):
    return jax.shard_map(
        shards,
        mesh=mesh,
        in_specs=(P("tm", None, "col"), P("tm", "col", None), P("tm", None, None), P()),
        out_specs=(P("tm", None, "col"), P("tm", None, "col"), P()),
        check_vma=False,
    )
```

time: 648 us -> 183 us (0.28)
  waiting for transfers between devices: 460 us -> 0 us
  Pallas kernels: 0 us -> 178 us
  blocking collectives: 75.9 us -> 0 us
  matrix products: 57.4 us -> 0 us
  starting transfers between devices: 19.8 us -> 0 us
  local copies, waits for them, and re-layouts: 17.9 us -> 3.57 us
  between operations: 14.2 us -> 0.65 us
    all_gather x14 -> x0, waiting for transfers between devices: 282 us -> none  [the longest x6 104 us: shards(): lax.all_gather(later_s, 'col', axis=1, tiled=True)]
    pallas_call x0 -> x1, Pallas kernels: none -> 178 us  [shards(): pl.pallas_call(functools.partial(kernel, groups), out_shape=(jax.ShapeDty...]
    ppermute x12 -> x0, waiting for transfers between devices: 177 us -> none  [passed_along(): return lax.ppermute(array, axis, pairs)]
    psum x1 -> x0, blocking collectives: 75.9 us -> none  [shards(): corner = corner_base + lax.psum(corner_term, ('tm', 'col')) / time_total]
    dot_general x16 -> x0, matrix products: 57.4 us -> none  [the longest x8 38.4 us: transposed_dot(): lax.dot_general(left, right, (((0,), (0,)), ((), ())), preferred_element_...]
    ppermute x12 -> x0, starting transfers between devices: 19.1 us -> none  [passed_along(): return lax.ppermute(array, axis, pairs)]
  transfers between devices with their start and end apart: 26 -> 0, of which waited for: 26 -> 0; matrix products, arithmetic and copies ran while one was open for 8% -> 0% of each run, Pallas kernels for 0% -> 0%
where the time goes in v2:
time: 183 us
  Pallas kernels  178 us (97%)
  local copies, waits for them, and re-layouts  3.57 us (2%)
    pallas_call x1, Pallas kernels, shards(): pl.pallas_call(functools.partial(kernel, groups), out_shape=(jax.ShapeDty...  178 us

profile of v2, /device:TPU:1, one launch (start us, length us, event | category | flops | bytes accessed | tf_op | source)
XLA Modules:
  0.0 182.6 jit_solution(16327834376603445370)
XLA Ops:
  0.6 178.4 %shard_map.67 = (bf16[2,1024,256]{2,1,0:T(8,128)(2,1)}, bf16[2,16,256]{2,1,0:T(8,128)(2,1)}, f32[16,16]{1,0:T(8,128)}) custom-call(bf16[2,1024,256]{2,1,0:T(8,128)(2,1)} %D.1, bf16[2,256,1024]{2,1,0:T(8,128)(2,1)} %G.1, bf16[2,16,1024]{2,1,0:T(8,128)(2,1)} %R.1, f32[16,16]{1,0:T(8,128)} %cb.1), custom_call_target="tpu_custom_call" | custom-call | flops 11811160064 | bytes 4194304 | tf_op jit(solution)/shard_map/pallas_call | solution.py:442
  179.0 0.0 copy-start
  179.1 2.3 %copy.10 = bf16[2,1024,256]{2,1,0:T(8,128)(2,1)} copy(bf16[2,1024,256]{2,1,0:T(8,128)(2,1)} %get-tuple-element.6) | data formatting | bytes 2097152
  181.3 0.0 copy-done
  181.3 0.0 copy-start.1
  181.3 0.6 copy.11
  181.9 0.1 copy-done.1
  182.0 0.6 copy.12
Async XLA Ops:
  179.0 2.3 %copy-start = (bf16[2,16,256]{2,1,0:T(8,128)(2,1)S(1)}, bf16[2,16,256]{2,1,0:T(8,128)(2,1)}, u32[]{:S(2)}) copy-start(bf16[2,16,256]{2,1,0:T(8,128)(2,1)} %get-tuple-element.7) | copy-start | bytes 49156
  181.3 0.7 copy-start.1

commit v3 on v2

--- a/solution.py
+++ b/solution.py
@@ -11,8 +11,9 @@
 BF16 = jnp.bfloat16
 F32 = jnp.float32
 X = 4
-CHUNKS = 2
-SEMS = 190
+PARTS = (1, 1, 1, 2, 2, 1)
+SEMS = 159
+FIRST = (0, 1, 2)
 
 
 def dot(a, b):
@@ -58,12 +59,11 @@
 
 
 def kernel(groups, D, G, R, cb, sig, arrow, corner,
-           GF, HA, HB, HC, HF, A, LA, LH, PS, PC, DC, DR, SB, RR, OT, C1, C2, C3, sems):
+           GF, HA, HB, HC, H0, HF, A, LA, LH, PS, PC, DC, DR, SB, RR, OT, C1, C2, C3, sems):
     n, w = D.shape[1], D.shape[2]
     h = n // 2
     m = w // 2
     hm = m // 2
-    cm = m // CHUNKS
     levels = groups.bit_length() - 1
     gy = min(4, groups)
     gz = groups // gy
@@ -100,6 +100,8 @@
         return pl.ds(pl.multiple_of(chip * w, w), w)
 
     mine = rows(me)
+    my_rows = pl.ds(pl.multiple_of(i * h, h), h)
+    its_rows = pl.ds(pl.multiple_of((1 - i) * h, h), h)
     my_lanes = pl.ds(pl.multiple_of(i * m, m), m)
     its_lanes = pl.ds(pl.multiple_of((1 - i) * m, m), m)
 
@@ -165,25 +167,35 @@
                     self.share(ref)
             links.wait(self.buf.at[pl.ds(0, (4 if self.own else 3) * m)], self.near)
 
+    t_sent = links.take()
+
     class Turn:
         def __init__(self, stage, buf, parts):
             self.stage, self.buf, self.parts = stage, buf, parts
-            self.sent, self.got = links.take(), links.take()
-            links.later(stage.at[pl.ds(0, 2 * X - 1)], self.sent)
-
-        def send(self, part, value):
+            self.sent, self.got = t_sent, links.take()
+
+        def send(self, part, value, half=None):
             size = m // self.parts
             at = pl.ds(part * size, size)
             value = value.astype(BF16)
-            for b in range(2 * X):
-                self.stage[b, at] = value[:, b * m:(b + 1) * m]
             to = pl.ds(pl.multiple_of(me * m + part * size, size), size)
-            for chip, c in ring:
-                links.copy(self.stage.at[2 * chip + c, at], self.buf.at[to], self.sent, self.got,
-                           2 * q + c, chip)
-            links.copy(self.stage.at[2 * x + 1 - i, at], self.buf.at[to], self.sent, self.got,
-                       sib, x)
-            self.buf[to] = self.stage[me, at]
+            if half is None:
+                for b in range(2 * X):
+                    self.stage[b, at] = value[:, b * m:(b + 1) * m]
+                for chip, c in ring + [(x, 1 - i)]:
+                    links.copy(self.stage.at[2 * chip + c, at], self.buf.at[to], self.sent,
+                               self.got, 2 * q + c, chip)
+                self.buf[to] = self.stage[me, at]
+                return
+            for b in range(X):
+                self.stage[X * half + b, at] = value[:, b * m:(b + 1) * m]
+            for b in range(X * half, X * half + X):
+                links.copy(self.stage.at[b, at], self.buf.at[to], self.sent, self.got,
+                           2 * q + b % 2, b // 2, b != me)
+
+            @pl.when(me // X == half)
+            def _():
+                self.buf[to] = self.stage[me, at]
 
         def receive(self):
             links.wait(self.buf.at[pl.ds(0, (2 * X - 1) * m)], self.got)
@@ -228,8 +240,8 @@
             at = rows(4 * i + j)
             out[at] = dot(L[at], H[...]).astype(BF16)
             links.copy(out.at[at], out.at[at], sent, got, sib, x)
-        links.later(out.at[pl.ds(pl.multiple_of(i * h, h), h)], sent)
-        return lambda: links.wait(out.at[pl.ds(pl.multiple_of((1 - i) * h, h), h)], got)
+        links.later(out.at[my_rows], sent)
+        return lambda: links.wait(out.at[its_rows], got)
 
     first0 = i == 0
     links.wait(GF.at[2 * i, panel(x)], g_here)
@@ -256,17 +268,6 @@
     SB[0] = (DR[1].astype(F32) + dot(turn_b.turned(), GF[2])).astype(BF16)
     gather1.mid()
     rows1 = Rows(1, 0, DR.at[0]).start()
-    gather1.end()
-    got_ha = whole_product(HA, GF.at[1], GF.at[0])
-    rows1.receive()
-    turn_a = turn_of(dot(DR[0], GF[0]))
-    got_ha()
-    turn = turn_of(dot(SB[0], HA[...]))
-    HF[0, mine] = dot(Hb, HA[...]).astype(BF16)
-    gather = Gather(HF.at[0]).start()
-    turn_a.receive()
-    Sa = (column(0) + dot(turn_a.turned(), GF[0])).astype(BF16)
-
     def later_start(src, buf, e, keep, want, parts):
         sent, got, size = links.take(), links.take(parts), m // parts
         for c in range(parts):
@@ -280,52 +281,129 @@
 
         return lambda c: links.wait(buf.at[pl.ds(c * size, size)], got + c, want)
 
-    def send_state(src, buf, e):
-        return later_start(src, buf, e, q >= e, q + e < groups, CHUNKS)
-
-    def send_map(src, buf, e):
-        return later_start(src, buf, e, jnp.logical_and(q >= e, q + e < groups),
-                           q + 2 * e < groups, 1)
-
-    def apply_later(got, L, H):
-        turn = new_turn(CHUNKS)
-        for c in range(CHUNKS):
-            got(c)
-            turn.send(c, dot(L[pl.ds(c * cm, cm)], H[...]))
-        return turn
-
-    got_h = send_map(HF.at[0, mine], LH.at[0], 1) if levels > 1 else None
-    gather.mid()
+    def send_state(k):
+        e = 1 if k == levels else 1 << k
+        return later_start(A.at[k], LA.at[k], e, q >= e, q + e < groups, PARTS[k])
+
+    def send_map(k, half):
+        e = 1 << k
+        return later_start(HF.at[k, half, mine] if k else H0.at[half], LH.at[k, :, pl.ds(half * h, h)], e,
+                           jnp.logical_and(q >= e, q + e < groups), q + 2 * e < groups, 1)
+
+    gather1.end()
+    gather3 = Gather(GF.at[3], False).start()
+    rows1.receive()
+    turn_a = turn_of(dot(DR[0], GF[0]))
+    whole_product(HA, GF.at[1], GF.at[0])()
+    turn = turn_of(dot(SB[0], HA[...]))
+    for half in (0, 1):
+        H0[half] = dot(Hb, HA[:, half * h:half * h + h]).astype(BF16)
+    got_h = [send_map(0, half) for half in (0, 1)] if levels > 1 else []
+    turn_a.receive()
+    Sa = (column(0) + dot(turn_a.turned(), GF[0])).astype(BF16)
+    gather3.mid()
     turn.receive()
     A[0] = (Sa.astype(F32) + dot(turn.turned(), HA[...])).astype(BF16)
-    got_a = send_state(A.at[0], LA.at[0], 1)
+    got_a = send_state(0)
     own = turn_of(A[0])
+    turn_c = turn_of(dot(SB[0], GF[1]))
+    turn_s = turn_of(SB[0])
+    gather3.end()
+    got_hb = whole_product(HB, GF.at[3], GF.at[2])
+    sent, got = links.take(), links.take()
+    for j in range(4):
+        at = rows(4 * i + j)
+        for half in (0, 1):
+            HF[0, half, at] = dot(HB[at], HA[:, half * h:half * h + h]).astype(BF16)
+        links.copy(HF.at[0, :, at], HF.at[0, :, at], sent, got, sib, x)
+    links.later(HF.at[0, :, my_rows], sent)
+    links.wait(HF.at[0, :, its_rows], got)
+    gathers = []
+    def small(a, b, dims):
+        return lax.dot_general(a, b, (dims, ((), ())), precision=lax.Precision.HIGHEST,
+                               preferred_element_type=F32)
+
+    def by_lanes(a, b):
+        return lax.dot_general(a, b, (((1,), (1,)), ((), ())), preferred_element_type=F32)
+
+    ar = R.shape[1]
+    maps = {3: GF.at[3], 2: HB, 1: HC}
+    ready = {}
+
+    def prepare(k):
+        if k == max(levels - 2, 0):
+            got_hb()
+            ready["hc"] = whole_product(HC, HB, GF.at[1])
+        if k == levels - 1:
+            ready["hc"]()
+            turn_c.receive()
+            SB[1] = (column(1) + dot(turn_c.turned(), GF[1])).astype(BF16)
+            turn_s.receive()
+            ready["own"] = {3: DC[3].T, 2: turn_s.turned(), 1: SB[1]}
+            lanes = [RR[t, :, pl.ds(pl.multiple_of(me * m, m), m)].astype(F32)
+                     for t in range(4)]
+            ready["lanes"] = lanes[0]
+            ready["total"] = sum(
+                small(by_lanes(ready["own"][t], RR[t]), lanes[t], ((0,), (1,)))
+                for t in (1, 2, 3))
+            ready["V"] = {t: by_lanes(RR[t], maps[t][mine]) for t in (1, 2, 3)}
+
     for k in range(levels):
         final = k + 1 == levels
-        e = 1 << k
-        gather.end()
+        ends, gathers, got = gathers, [], []
+        def compose(half):
+            HF[k + 1, half, mine] = dot(LH[k], HF[k, half]).astype(BF16)
+            gathers.append(Gather(HF.at[k + 1, half]).start())
+            if k + 2 < levels:
+                got.append(send_map(k + 1, half))
+
+        def apply():
+            size = m // PARTS[k]
+            for c in range(PARTS[k]):
+                got_a(c)
+                for half in (0, 1):
+                    turn.send(c, dot(LA[k, pl.ds(c * size, size)], HF[k, half]), half)
+
+        turn = new_turn(PARTS[k])
+        if k == 0:
+            apply()
+            if not final:
+                for received in got_h:
+                    received(0)
+                compose(0)
+                compose(1)
+        else:
+            ends[0].end()
+            if not final:
+                for received in got_h:
+                    received(0)
+                compose(0)
+            ends[1].end()
+            if k not in FIRST and not final:
+                compose(1)
+            if k + 1 >= levels - 1:
+                prepare(k)
+            apply()
+            if k in FIRST and not final:
+                compose(1)
+        got_h = got
         if not final:
-            got_h(0)
-            HF[k + 1, mine] = dot(LH[k], HF[k]).astype(BF16)
-            gather = Gather(HF.at[k + 1]).start()
-            if k + 2 < levels:
-                got_h = send_map(HF.at[k + 1, mine], LH.at[k + 1], 2 * e)
-        else:
-            gather = gather3 = Gather(GF.at[3], False).start()
-            gather3.mid()
-        turn = apply_later(got_a, LA.at[k], HF.at[k])
-        if final:
-            turn_c = turn_of(dot(SB[0], GF[1]))
-            turn_s = turn_of(SB[0])
-        else:
-            gather.mid()
+            gathers[0].mid()
+        if k + 2 == levels:
+            gathers[1].mid()
         own.receive()
         before = own.turned().astype(F32)
         turn.receive()
-        A[k + 1] = (before + dot(turn.turned(), HF[k])).astype(BF16)
-        got_a = send_state(A.at[k + 1], LA.at[k + 1], 1 if final else 2 * e)
+        columns = turn.turned()
+        for half in (0, 1):
+            at = pl.ds(half * h, h)
+            A[k + 1, :, at] = (before[:, half * h:half * h + h]
+                               + dot(columns, HF[k, half])).astype(BF16)
+        got_a = send_state(k + 1)
         if not final:
             own = turn_of(A[k + 1])
+            if k + 2 != levels:
+                gathers[1].mid()
 
     class RowsOut:
         def __init__(self, src, core, s):
@@ -372,53 +450,41 @@
                 out += self.buf[k]
             return out
 
-    def small(a, b, dims):
-        return lax.dot_general(a, b, (dims, ((), ())), precision=lax.Precision.HIGHEST,
-                               preferred_element_type=F32)
-
-    def by_lanes(a, b):
-        return lax.dot_general(a, b, (((1,), (1,)), ((), ())), preferred_element_type=F32)
-
+    if levels == 1:
+        prepare(0)
     out0 = RowsOut(A.at[levels], 0, 0)
-    gather3.end()
-    got_hb = whole_product(HB, GF.at[3], GF.at[2])
-    got_hb()
-    got_hc = whole_product(HC, HB, GF.at[1])
-    turn_c.receive()
-    SB[1] = (column(1) + dot(turn_c.turned(), GF[1])).astype(BF16)
-    turn_s.receive()
-    own_terms = {3: DC[3].T, 2: turn_s.turned(), 1: SB[1]}
-    maps = {3: GF.at[3], 2: HB, 1: HC}
-    ar = R.shape[1]
-    my_arrow = [RR[t, :, pl.ds(pl.multiple_of(me * m, m), m)].astype(F32) for t in range(4)]
-    total = small(my_arrow[0], by_lanes(A[levels], RR[0]), ((1,), (0,)))
+    own_terms, V = ready["own"], ready["V"]
+    total = ready["total"] + small(ready["lanes"], by_lanes(A[levels], RR[0]), ((1,), (0,)))
+    turns_out = {t: new_turn(PARTS[levels]) for t in (3, 2, 1)}
+    assert PARTS[levels] == 1
+    got_a(0)
+    products = {}
+    for t in (3, 2, 1):
+        products[t] = dot(LA[levels], maps[t][...]).astype(BF16)
+        if t == 3:
+            turns_out[t].send(0, products[t])
     for t in (1, 2, 3):
-        total += small(by_lanes(own_terms[t], RR[t]), my_arrow[t], ((0,), (1,)))
-    got_hc()
-    V = {t: by_lanes(RR[t], maps[t][mine]) for t in (1, 2, 3)}
-    turns_out = {t: new_turn(CHUNKS) for t in (3, 2, 1)}
-    products = []
-    for c in range(CHUNKS):
-        got_a(c)
-        for t in (3, 2, 1):
-            product = dot(LA[levels, pl.ds(c * cm, cm)], maps[t][...]).astype(BF16)
-            turns_out[t].send(c, product)
-            products.append((t, c, product))
-    for t, c, product in products:
-        total += small(V[t][:, c * cm:(c + 1) * cm], by_lanes(product, RR[t]), ((1,), (0,)))
+        total += small(V[t], by_lanes(products[t], RR[t]), ((1,), (0,)))
     total = jnp.concatenate([total, jnp.zeros((ar, C1.shape[2] - ar), F32)], axis=1)
-    total = Sum(C1, me, total, [(sib, x)] + [(2 * q + c, chip) for chip, c in ring]).receive()
-    if gy > 1:
-        total = Sum(C2, qy, total, [(2 * g + i, x) for g in ys]).receive()
-    if gz > 1:
-        corner_sum = Sum(C3, qz, total, [(2 * g + i, x) for g in zs])
+    corner_sum = Sum(C1, me, total, [(sib, x)] + [(2 * q + c, chip) for chip, c in ring])
+    for t in (2, 1):
+        turns_out[t].send(0, products[t])
 
     def sigma_of(t):
         turns_out[t].receive()
         value = (own_terms[t].astype(F32) + dot(turns_out[t].turned(), maps[t][...])).astype(BF16)
         return ColumnsOut(OT.at[t - 1], value, t // 2, t % 2)
 
-    outs = [out0, sigma_of(3), sigma_of(2), sigma_of(1)]
+    outs = [out0]
+    total = corner_sum.receive()
+    if gy > 1:
+        corner_sum = Sum(C2, qy, total, [(2 * g + i, x) for g in ys])
+    outs += [sigma_of(3), sigma_of(2)]
+    if gy > 1:
+        total = corner_sum.receive()
+    if gz > 1:
+        corner_sum = Sum(C3, qz, total, [(2 * g + i, x) for g in zs])
+    outs.append(sigma_of(1))
     for out in outs:
         out.receive()
     for s in (0, 1):
@@ -426,7 +492,14 @@
     if gz > 1:
         total = corner_sum.receive()
     corner[...] = cb[...] + total[:, :ar] / (4 * groups)
+    links.later(PS.at[pl.ds(0, turns[0]), pl.ds(0, 2 * X - 1)], t_sent)
     links.drain()
+
+
+def passed_on(*refs):
+    count = len(refs) // 2
+    for src, dst in zip(refs[:count], refs[count:]):
+        dst[...] = src[...]
 
 
 def shards(precision_blocks, coupling, arrow_rows, corner_base):
@@ -435,17 +508,18 @@
     assert levels % 2 == 1
     n, w = precision_blocks.shape[1:]
     ar = arrow_rows.shape[1]
-    m = w // 2
+    h, m = n // 2, w // 2
     vmem = pl.BlockSpec(memory_space=pltpu.VMEM)
     far = pl.BlockSpec(memory_space=pl.ANY)
     turns = 2 * levels + 8
-    return pl.pallas_call(
+    shapes = (
+        jax.ShapeDtypeStruct(precision_blocks.shape, BF16),
+        jax.ShapeDtypeStruct((2, ar, w), BF16),
+        jax.ShapeDtypeStruct((ar, ar), F32),
+    )
+    results = pl.pallas_call(
         functools.partial(kernel, groups),
-        out_shape=(
-            jax.ShapeDtypeStruct(precision_blocks.shape, BF16),
-            jax.ShapeDtypeStruct((2, ar, w), BF16),
-            jax.ShapeDtypeStruct((ar, ar), F32),
-        ),
+        out_shape=shapes,
         in_specs=[far, far, far, vmem],
         out_specs=(vmem,) * 3,
         scratch_shapes=[
@@ -453,7 +527,8 @@
             pltpu.VMEM((n, n), BF16),
             pltpu.VMEM((n, n), BF16),
             pltpu.VMEM((n, n), BF16),
-            pltpu.VMEM((levels, n, n), BF16),
+            pltpu.VMEM((2, m, n // 2), BF16),
+            pltpu.VMEM((levels, 2, n, h), BF16),
             pltpu.VMEM((levels + 1, m, n), BF16),
             pltpu.VMEM((levels + 1, m, n), BF16),
             pltpu.VMEM((levels, m, n), BF16),
@@ -474,6 +549,12 @@
         cost_estimate=pl.CostEstimate(
             flops=2 * 22 * w * n * n, bytes_accessed=4 << 20, transcendentals=0),
     )(precision_blocks, coupling, arrow_rows, corner_base)
+    return pl.pallas_call(
+        passed_on,
+        out_shape=shapes,
+        in_specs=[vmem] * 3,
+        out_specs=(vmem,) * 3,
+    )(*results)
 
 
 def solution(mesh):

time: 183 us -> 172 us (0.940)
  Pallas kernels: 178 us -> 171 us
  local copies, waits for them, and re-layouts: 3.57 us -> 0 us
    pallas_call x1 -> x2, Pallas kernels: 178 us -> 171 us  [the longest x1 169 us: shards(): pl.pallas_call(functools.partial(kernel, groups), out_shape=shapes, in_sp...]
    unnamed x7 -> x0, local copies, waits for them, and re-layouts: 3.57 us -> none
where the time goes in v3:
time: 172 us
  Pallas kernels  171 us (99%)
    pallas_call x1, Pallas kernels, shards(): pl.pallas_call(functools.partial(kernel, groups), out_shape=shapes, in_sp...  169 us

profile of v3, /device:TPU:1, one launch (start us, length us, event | category | flops | bytes accessed | tf_op | source)
XLA Modules:
  0.0 172.0 jit_solution(16014391417255572796)
XLA Ops:
  0.6 169.1 %shard_map.67 = (bf16[2,1024,256]{2,1,0:T(8,128)(2,1)}, bf16[2,16,256]{2,1,0:T(8,128)(2,1)}, f32[16,16]{1,0:T(8,128)}) custom-call(bf16[2,1024,256]{2,1,0:T(8,128)(2,1)} %D.1, bf16[2,256,1024]{2,1,0:T(8,128)(2,1)} %G.1, bf16[2,16,1024]{2,1,0:T(8,128)(2,1)} %R.1, f32[16,16]{1,0:T(8,128)} %cb.1), custom_call_target="tpu_custom_call" | custom-call | flops 11811160064 | bytes 4194304 | tf_op jit(solution)/shard_map/pallas_call | solution.py:520
  169.7 2.3 %shard_map.68 = (bf16[2,1024,256]{2,1,0:T(8,128)(2,1)}, bf16[2,16,256]{2,1,0:T(8,128)(2,1)}, f32[16,16]{1,0:T(8,128)}) custom-call(bf16[2,1024,256]{2,1,0:T(8,128)(2,1)} %get-tuple-element.6.refs_0_, bf16[2,16,256]{2,1,0:T(8,128)(2,1)} %get-tuple-element.7.refs_1_, f32[16,16]{1,0:T(8,128)} %get-tuple-element.8.refs_2_), custom_call_target="tpu_custom_call" | custom-call | tf_op jit(solution)/shard_map/pallas_call | solution.py:552

commit v4 on v3

--- a/solution.py
+++ b/solution.py
@@ -11,8 +11,8 @@
 BF16 = jnp.bfloat16
 F32 = jnp.float32
 X = 4
-PARTS = (1, 1, 1, 2, 2, 1)
-SEMS = 159
+PARTS = (1, 1, 1, 2, 2, 2)
+SEMS = 160
 FIRST = (0, 1, 2)
 
 
@@ -456,19 +456,22 @@
     own_terms, V = ready["own"], ready["V"]
     total = ready["total"] + small(ready["lanes"], by_lanes(A[levels], RR[0]), ((1,), (0,)))
     turns_out = {t: new_turn(PARTS[levels]) for t in (3, 2, 1)}
-    assert PARTS[levels] == 1
-    got_a(0)
-    products = {}
-    for t in (3, 2, 1):
-        products[t] = dot(LA[levels], maps[t][...]).astype(BF16)
-        if t == 3:
-            turns_out[t].send(0, products[t])
-    for t in (1, 2, 3):
-        total += small(V[t], by_lanes(products[t], RR[t]), ((1,), (0,)))
+    lm = m // PARTS[levels]
+    for c in range(PARTS[levels]):
+        at = pl.ds(c * lm, lm)
+        got_a(c)
+        products = {}
+        for t in (3, 2, 1):
+            products[t] = dot(LA[levels, at], maps[t][...]).astype(BF16)
+            if c + 1 < PARTS[levels]:
+                turns_out[t].send(c, products[t])
+        for t in (1, 2, 3):
+            total += small(V[t][:, c * lm:c * lm + lm], by_lanes(products[t], RR[t]),
+                           ((1,), (0,)))
     total = jnp.concatenate([total, jnp.zeros((ar, C1.shape[2] - ar), F32)], axis=1)
     corner_sum = Sum(C1, me, total, [(sib, x)] + [(2 * q + c, chip) for chip, c in ring])
-    for t in (2, 1):
-        turns_out[t].send(0, products[t])
+    for t in (3, 2, 1):
+        turns_out[t].send(PARTS[levels] - 1, products[t])
 
     def sigma_of(t):
         turns_out[t].receive()

time: 172 us -> 170 us (0.988)
  no operation moved by 1% of the time
where the time goes in v4:
time: 170 us
  Pallas kernels  170 us (100%)
    pallas_call x1, Pallas kernels, shards(): pl.pallas_call(functools.partial(kernel, groups), out_shape=shapes, in_sp...  167 us

profile of v4, /device:TPU:1, one launch (start us, length us, event | category | flops | bytes accessed | tf_op | source)
XLA Modules:
  0.0 170.3 jit_solution(15672210773356809919)
XLA Ops:
  0.6 167.4 %shard_map.67 = (bf16[2,1024,256]{2,1,0:T(8,128)(2,1)}, bf16[2,16,256]{2,1,0:T(8,128)(2,1)}, f32[16,16]{1,0:T(8,128)}) custom-call(bf16[2,1024,256]{2,1,0:T(8,128)(2,1)} %D.1, bf16[2,256,1024]{2,1,0:T(8,128)(2,1)} %G.1, bf16[2,16,1024]{2,1,0:T(8,128)(2,1)} %R.1, f32[16,16]{1,0:T(8,128)} %cb.1), custom_call_target="tpu_custom_call" | custom-call | flops 11811160064 | bytes 4194304 | tf_op jit(solution)/shard_map/pallas_call | solution.py:523
  168.0 2.3 %shard_map.68 = (bf16[2,1024,256]{2,1,0:T(8,128)(2,1)}, bf16[2,16,256]{2,1,0:T(8,128)(2,1)}, f32[16,16]{1,0:T(8,128)}) custom-call(bf16[2,1024,256]{2,1,0:T(8,128)(2,1)} %get-tuple-element.6.refs_0_, bf16[2,16,256]{2,1,0:T(8,128)(2,1)} %get-tuple-element.7.refs_1_, f32[16,16]{1,0:T(8,128)} %get-tuple-element.8.refs_2_), custom_call_target="tpu_custom_call" | custom-call | tf_op jit(solution)/shard_map/pallas_call | solution.py:555
